TPU v7x, 256 devices: a whole 4x4x8 slice. The times are simulated.
256 devices in a mesh: band: 64 (over y, z, core), rep: 4 (over x).
Axes of the slice: x: 4, y: 4, z: 8, core: 2. Of those that a mesh axis runs over, the one named last changes fastest.
Arguments:
- embeddings: bfloat16 [128, 32768], P('rep', 'band'), may hold values from -6 to 6
- route: int32 [32768, 1], P('band'), may hold values from 0 to 63; in each aligned block of 512 rows (0 to 511, 512 to 1023, ...) at most 20 rows name the same one
- place: bfloat16 [2, 32768], P(None, 'band'), may hold values from 0 to 1
- scales: float32 [4], replicated, may hold values from 0.25 to 1
- first_weight: bfloat16 [512, 512], replicated, may hold values from -0.25 to 0.25
- first_bias: float32 [512], replicated, may hold values from -3 to 3
- second_weight: bfloat16 [512, 512], replicated, may hold values from -0.25 to 0.25
- out_cotangent: bfloat16 [512, 768, 256], P(None, ('band', 'rep')), may hold values from -6 to 6
Outputs:
- embed_gradient: float32 [128, 32768], P('rep', 'band')
- first_weight_gradient: float32 [512, 512], replicated
- first_bias_gradient: float32 [512], replicated
- second_weight_gradient: float32 [512, 512], replicated
Inputs may be any that keep to these rules, and one draw needn't show every extreme that they name: `route`: within the 512 reports of one feed (aligned blocks of rows), at most 20 name the same band, and in some block exactly 20 do.
All inputs are finite; a program needn't handle non-finite values.
Results may differ from a plain program's by a relative error of at most 0.0063.
Values may be sent and summed in bfloat16 or wider, within the bound.
A program may use at most 128 MiB of HBM per device.

v0:
```python
import jax
import jax.numpy as jnp
from jax import lax
from jax.sharding import PartitionSpec as P

root_two_pi = 0.7978845608028654
cubic = 0.044715


def gelu_value(value):
    inner = root_two_pi * (value + cubic * value * value * value)
    return 0.5 * value * (1.0 + jnp.tanh(inner))


def gelu_slope(value):
    tangent = jnp.tanh(root_two_pi * (value + cubic * value * value * value))
    return 0.5 * (1.0 + tangent) + 0.5 * value * (1.0 - tangent * tangent) * root_two_pi * (
        1.0 + 3.0 * cubic * value * value
    )


def kernel_factors(geometry, block, scales, lat_rows, columns):
    north_fraction = geometry[0]
    east_fraction = geometry[1]
    valid = geometry[2]
    centre_rows = jnp.arange(lat_rows, dtype=jnp.float32) + 0.5
    north_gap = (
        ((1 - block).astype(jnp.float32) * lat_rows)[None, :]
        + centre_rows[:, None]
        - (north_fraction * lat_rows)[None, :]
    )
    east_gap = (jnp.arange(columns, dtype=jnp.float32) + 0.5)[:, None] - (east_fraction * columns)[
        None, :
    ]
    reach = scales * lat_rows
    inverse = 0.5 / (reach * reach)
    row_kernel = (
        jnp.exp(-(north_gap * north_gap)[None] * inverse[:, None, None]) * valid[None, None, :]
    ).astype(jnp.bfloat16)
    column_kernel = jnp.exp(-(east_gap * east_gap)[None] * inverse[:, None, None]).astype(
        jnp.bfloat16
    )
    return (row_kernel, column_kernel)


def splat(embedded, row_kernel, column_kernel):
    channels = embedded.shape[0]
    levels, lat_rows, slots = row_kernel.shape
    columns = column_kernel.shape[1]
    sums = []
    weights = []
    for level in range(levels):
        weighted = (embedded[:, None, :] * row_kernel[level][None]).reshape(
            channels * lat_rows, slots
        )
        sums.append(
            lax.dot_general(
                weighted,
                column_kernel[level],
                (((1,), (1,)), ((), ())),
                preferred_element_type=jnp.float32,
            )
        )
        weights.append(
            lax.dot_general(
                row_kernel[level],
                column_kernel[level],
                (((1,), (1,)), ((), ())),
                preferred_element_type=jnp.float32,
            )
        )
    splatted = jnp.stack(sums).reshape(levels, channels, lat_rows * columns)
    density = jnp.stack(weights).reshape(levels, lat_rows * columns)
    features = (
        (splatted / (density[:, None, :] + 1.0))
        .transpose(1, 0, 2)
        .reshape(channels * levels, lat_rows * columns)
        .astype(jnp.bfloat16)
    )
    return (features, density)


def spread_back(gradient, row_kernel, column_kernel):
    levels, lat_rows, slots = row_kernel.shape
    columns = column_kernel.shape[1]
    channels = gradient.shape[0] // levels
    grid = gradient.reshape(channels, levels, lat_rows * columns)
    total = jnp.zeros((channels, slots), jnp.float32)
    for level in range(levels):
        slab = grid[:, level].reshape(channels * lat_rows, columns)
        along = jnp.dot(slab, column_kernel[level], preferred_element_type=jnp.float32).reshape(
            channels, lat_rows, slots
        )
        total = total + jnp.sum(along * row_kernel[level][None].astype(jnp.float32), axis=1)
    return total


def band_ranks(route_rows, bands):
    owner = route_rows[:, 0]
    onehot = (owner[:, None] == jnp.arange(bands, dtype=jnp.int32)[None, :]).astype(jnp.int32)
    running = jnp.cumsum(onehot, axis=0)
    return (owner, jnp.sum((running - 1) * onehot, axis=1))


def on_device(
    embeddings, route, place, scales, first_weight, first_bias, second_weight, out_cotangent
):
    channels, reports = embeddings.shape
    bands = lax.axis_size("band")
    parts = lax.axis_size("rep")
    quarter = lax.axis_index("rep")
    capacity = max(2, 5 * reports // (2 * bands))
    sub_rows = out_cotangent.shape[1]
    lat_rows = sub_rows * parts
    columns = out_cotangent.shape[2]
    levels = scales.shape[0]
    owner, rank = band_ranks(route, bands)
    packed = jnp.concatenate([embeddings, place, jnp.ones((1, reports), jnp.bfloat16)], axis=0)
    rows = channels + 3
    span = 3 * capacity
    outgoing = jnp.zeros((rows, bands * span), jnp.bfloat16)
    for offset in range(3):
        target = owner + 1 - offset
        inside = (target >= 0) & (target < bands)
        where_to = jnp.where(inside, target * span + offset * capacity + rank, bands * span)
        outgoing = outgoing.at[:, where_to].set(packed, mode="drop")
    nearby = lax.all_to_all(outgoing, "band", split_axis=1, concat_axis=1, tiled=True)
    block = jnp.arange(bands * span, dtype=jnp.int32) // capacity % 3
    geometry = nearby[channels:].astype(jnp.float32)
    row_kernel, column_kernel = kernel_factors(geometry, block, scales, lat_rows, columns)
    features, density = splat(nearby[:channels], row_kernel, column_kernel)
    cotangent = out_cotangent.reshape(out_cotangent.shape[0], sub_rows * columns)
    mine = lax.all_to_all(features, "rep", split_axis=1, concat_axis=0, tiled=True)
    local_density = lax.dynamic_slice_in_dim(
        density.reshape(levels, lat_rows, columns), quarter * sub_rows, sub_rows, 1
    ).reshape(levels, sub_rows * columns)
    preact = (
        lax.dot_general(
            first_weight, mine, (((0,), (0,)), ((), ())), preferred_element_type=jnp.float32
        )
        + first_bias[:, None]
    )
    hidden = gelu_value(preact).astype(jnp.bfloat16)
    pre_gradient = (
        jnp.dot(second_weight, cotangent, preferred_element_type=jnp.float32) * gelu_slope(preact)
    ).astype(jnp.bfloat16)
    first_sum = lax.dot_general(
        mine, pre_gradient, (((1,), (1,)), ((), ())), preferred_element_type=jnp.float32
    )
    second_sum = lax.dot_general(
        hidden, cotangent, (((1,), (1,)), ((), ())), preferred_element_type=jnp.float32
    )
    bias_sum = jnp.sum(pre_gradient.astype(jnp.float32), axis=1)
    feature_gradient = jnp.dot(first_weight, pre_gradient, preferred_element_type=jnp.float32)
    count = sub_rows * columns
    cell_part = (
        (feature_gradient.reshape(-1, levels, count) / (local_density[None] + 1.0))
        .reshape(-1, count)
        .astype(jnp.bfloat16)
    )
    splat_gradient = lax.all_to_all(cell_part, "rep", split_axis=0, concat_axis=1, tiled=True)
    totals = lax.psum((first_sum, second_sum, bias_sum), ("band", "rep"))
    slot_gradient = spread_back(splat_gradient, row_kernel, column_kernel)
    backward = lax.all_to_all(slot_gradient, "band", split_axis=1, concat_axis=1, tiled=True)
    embed_gradient = jnp.zeros((channels, reports), jnp.float32)
    for offset in range(3):
        target = owner + 1 - offset
        inside = (target >= 0) & (target < bands)
        where_from = jnp.where(inside, target * span + offset * capacity + rank, 0)
        embed_gradient = embed_gradient + jnp.where(inside[None, :], backward[:, where_from], 0.0)
    return (embed_gradient, totals[0], totals[2], totals[1])


def solution(mesh):
    return jax.shard_map(
        on_device,
        mesh=mesh,
        in_specs=(
            P("rep", "band"),
            P("band", None),
            P(None, "band"),
            P(),
            P(),
            P(),
            P(),
            P(None, ("band", "rep"), None),
        ),
        out_specs=(P("rep", "band"), P(), P(), P()),
        check_vma=False,
    )
```

profile of v0, /device:TPU:1, one launch (start us, length us, event | category | flops | bytes accessed | tf_op | source)
XLA Modules:
  0.0 442.8 jit_solution(7938262040771985791)
XLA Ops:
  21.7 13.4 %all-to-all-start = ((bf16[64,2,1050]{2,1,0:T(2,128)(2,1)}), bf16[64,2,1050]{2,1,0:T(2,128)(2,1)S(1)}, u32[]{:S(2)}, u32[]{:S(2)}) async-start(bf16[64,2,1050]{2,1,0:T(2,128)(2,1)} %reshape.419), calls=%async_computation | async-start | bytes 589824 | tf_op jit(solution)/shard_map/all_to_all | solution.py:127
  35.2 12.5 %all-to-all-done = bf16[64,2,1050]{2,1,0:T(2,128)(2,1)S(1)} async-done(((bf16[64,2,1050]{2,1,0:T(2,128)(2,1)}), bf16[64,2,1050]{2,1,0:T(2,128)(2,1)S(1)}, u32[]{:S(2)}, u32[]{:S(2)}) %all-to-all-start) | async-done | bytes 268832 | tf_op jit(solution)/shard_map/all_to_all | solution.py:127
  51.8 2.9 exponential_convert_fusion
  59.5 6.8 %broadcast_multiply_fusion.3 = (bf16[32,12,3840]{2,1,0:T(8,128)(2,1)}, bf16[32,12,3840]{2,1,0:T(8,128)(2,1)}, bf16[32,12,3840]{2,1,0:T(8,128)(2,1)}, bf16[32,12,3840]{2,1,0:T(8,128)(2,1)}) fusion(bf16[12,3840]{1,0:T(8,128)(2,1)} %get-tuple-element.32, bf16[32,3840]{1,0:T(8,128)(2,1)S(1)} %mul.298, bf16[12,3840]{1,0:T(8,128)(2,1)} %get-tuple-element.31, ...), kind=kLoop, calls=%fused_computation.37 | loop fusion | flops 5898240 | bytes 12410880 | tf_op jit(solution)/shard_map/mul | solution.py:53
  66.3 3.9 mul.315
  70.2 3.3 fusion.18
  75.6 3.9 mul.326
  79.5 3.3 fusion.14
  84.9 3.9 mul.330
  88.8 3.2 fusion.10
  94.2 4.1 mul.334
  98.3 3.2 fusion.6
  103.1 2.8 fusion.54
  107.1 4.0 all-to-all-start.1
  114.3 8.5 %all-to-all-done.1 = bf16[128,4,768]{2,0,1:T(8,128)(2,1)S(1)} async-done(((bf16[128,4,768]{2,0,1:T(8,128)(2,1)}), bf16[128,4,768]{2,0,1:T(8,128)(2,1)S(1)}, u32[]{:S(2)}, u32[]{:S(2)}) %all-to-all-start.1) | async-done | bytes 786464 | tf_op jit(solution)/shard_map/all_to_all | solution.py:133
  126.9 3.9 all-to-all-start.2
  130.8 3.0 fusion.53
  133.9 7.3 %all-to-all-done.2 = bf16[4,128,768]{2,1,0:T(8,128)(2,1)S(1)} async-done(((bf16[4,128,768]{2,1,0:T(8,128)(2,1)}), bf16[4,128,768]{2,1,0:T(8,128)(2,1)S(1)}, u32[]{:S(2)}, u32[]{:S(2)}) %all-to-all-start.2) | async-done | bytes 786464 | tf_op jit(solution)/shard_map/all_to_all | solution.py:161
  142.1 3.4 slice_reduce_fusion.2
  145.5 2.7 fusion.23
  157.8 8.0 %all-to-all-start.3 = ((f32[64,1,1920]{2,1,0:T(1,128)}), f32[64,1,1920]{2,1,0:T(1,128)S(1)}, u32[]{:S(2)}, u32[]{:S(2)}) async-start(f32[64,1,1920]{2,1,0:T(1,128)} %reshape.421), calls=%async_computation.3 | async-start | bytes 983040 | tf_op jit(solution)/shard_map/all_to_all | solution.py:164
  165.8 2.7 fusion.90
  168.6 76.4 %psum.22 = f32[512]{0:T(512)} all-reduce(f32[512]{0:T(512)S(1)} %get-tuple-element.46), channel_id=1, replica_groups=mesh['band'=64,'rep'=4] {'band','rep'}, use_global_device_ids=true, to_apply=%region_12.13 | all-reduce | flops 512 | bytes 4096 | tf_op jit(solution)/shard_map/psum | solution.py:162
  254.8 177.7 %all-reduce.3.cloned.1.call-done = (f32[512,512]{1,0:T(8,128)}, f32[512,512]{1,0:T(8,128)}) async-done(((f32[512,512]{1,0:T(8,128)}, f32[512,512]{1,0:T(8,128)}), (f32[512,512]{1,0:T(8,128)}, f32[512,512]{1,0:T(8,128)})) %all-reduce.3.cloned.1.call-update) | async-done | bytes 2097168 | tf_op jit(solution)/shard_map/psum | solution.py:162
  (124 shorter events, 63.3 us)
Async XLA Ops:
  7.2 115.7 %copy-start = (bf16[512,512]{1,0:T(8,128)(2,1)S(1)}, bf16[512,512]{1,0:T(8,128)(2,1)}, u32[]{:S(2)}) copy-start(bf16[512,512]{1,0:T(8,128)(2,1)} %param.12) | copy-start | bytes 1572868
  19.1 16.2 %copy-start.15 = (f32[4]{0:T(128)S(1)}, f32[4]{0:T(128)}, u32[]{:S(2)}) copy-start(f32[4]{0:T(128)} %param.11) | copy-start | bytes 52
  21.7 26.0 %all-to-all-start = ((bf16[64,2,1050]{2,1,0:T(2,128)(2,1)}), bf16[64,2,1050]{2,1,0:T(2,128)(2,1)S(1)}, u32[]{:S(2)}, u32[]{:S(2)}) async-start(bf16[64,2,1050]{2,1,0:T(2,128)(2,1)} %reshape.419), calls=%async_computation | async-start | bytes 589824 | tf_op jit(solution)/shard_map/all_to_all | solution.py:127
  49.4 0.8 copy-start.2
  54.7 3.1 copy-start.1
  54.8 1.7 copy-start.3
  106.1 5.0 %copy-start.6 = (bf16[512,3,256]{2,0,1:T(8,128)(2,1)S(1)}, bf16[512,3,256]{2,0,1:T(8,128)(2,1)}, u32[]{:S(2)}) copy-start(bf16[512,3,256]{2,0,1:T(8,128)(2,1)} %param.15) | copy-start | bytes 2359300
  107.1 15.7 %all-to-all-start.1 = ((bf16[128,4,768]{2,0,1:T(8,128)(2,1)}), bf16[128,4,768]{2,0,1:T(8,128)(2,1)S(1)}, u32[]{:S(2)}, u32[]{:S(2)}) async-start(bf16[128,4,768]{2,0,1:T(8,128)(2,1)} %copy.51), calls=%async_computation.1 | async-start | bytes 1572864 | tf_op jit(solution)/shard_map/all_to_all | solution.py:133
  112.5 10.3 %copy-start.14 = (f32[512]{0:T(512)S(1)}, f32[512]{0:T(512)}, u32[]{:S(2)}) copy-start(f32[512]{0:T(512)} %param.13) | copy-start | bytes 6148
  114.3 9.2 %copy-start.7 = (bf16[512,3,256]{0,2,1:T(8,128)(2,1)S(1)}, bf16[512,3,256]{0,2,1:T(8,128)(2,1)}, u32[]{:S(2)}) copy-start(bf16[512,3,256]{0,2,1:T(8,128)(2,1)} %copy.39) | copy-start | bytes 2359300
  114.3 9.2 %copy-start.13 = (bf16[512,512]{1,0:T(8,128)(2,1)S(1)}, bf16[512,512]{1,0:T(8,128)(2,1)}, u32[]{:S(2)}) copy-start(bf16[512,512]{1,0:T(8,128)(2,1)} %param.14) | copy-start | bytes 1572868
  123.5 1.4 copy-start.16
  123.5 2.0 copy-start.4
  124.8 2.1 copy-start.8
  126.9 14.2 %all-to-all-start.2 = ((bf16[4,128,768]{2,1,0:T(8,128)(2,1)}), bf16[4,128,768]{2,1,0:T(8,128)(2,1)S(1)}, u32[]{:S(2)}, u32[]{:S(2)}) async-start(bf16[4,128,768]{2,1,0:T(8,128)(2,1)} %bitcast.182), calls=%async_computation.2 | async-start | bytes 1572864 | tf_op jit(solution)/shard_map/all_to_all | solution.py:161
  142.1 8.7 %slice-start = ((s8[7864320]{0:T(1024)(128)(4,1)}), s8[3670016]{0:T(1024)(128)(4,1)S(1)}, s32[]{:S(2)}) async-start(s8[7864320]{0:T(1024)(128)(4,1)} %bitcast.170), calls=%async_computation.5 | async-start | bytes 7340032
  145.5 2.7 copy-start.11
  145.5 5.3 %slice-start.1 = ((s8[7864320]{0:T(1024)(128)(4,1)}), s8[4194304]{0:T(1024)(128)(4,1)S(1)}, s32[]{:S(2)}) async-start(s8[7864320]{0:T(1024)(128)(4,1)} %bitcast.170), calls=%async_computation.6 | async-start | bytes 8388608
  148.2 2.6 copy-start.10
  150.9 1.0 copy-start.9
  157.8 87.2 %all-to-all-start.3 = ((f32[64,1,1920]{2,1,0:T(1,128)}), f32[64,1,1920]{2,1,0:T(1,128)S(1)}, u32[]{:S(2)}, u32[]{:S(2)}) async-start(f32[64,1,1920]{2,1,0:T(1,128)} %reshape.421), calls=%async_computation.3 | async-start | bytes 983040 | tf_op jit(solution)/shard_map/all_to_all | solution.py:164
  165.7 2.8 copy-start.12
  165.7 266.8 %all-reduce.3.cloned.1.call-start = ((), (), s32[]{:S(2)}) async-start(), calls=%async_computation.4 | async-start | bytes 4194304 | tf_op jit(solution)/shard_map/psum | solution.py:162
  432.5 2.4 copy-start.5
Sparse Core Ops, SparseCore 0:
  172.7 259.7 all-reduce.2
where the time goes:
time: 451 us; the launch traced here: 443 us
  waiting for transfers between devices  206 us (46%)
  blocking collectives  76.4 us (17%)
  local copies, waits for them, and re-layouts  61.9 us (14%)
  matrix products  33 us (7%)
  starting transfers between devices  29.4 us (7%)
  other arithmetic  21.3 us (5%)
  between operations  14.9 us (3%)
    psum x1, waiting for transfers between devices, on_device(): totals = lax.psum((first_sum, second_sum, bias_sum), ('band', 'rep'))  178 us
    psum x1, blocking collectives, on_device(): totals = lax.psum((first_sum, second_sum, bias_sum), ('band', 'rep'))  76.4 us
    mul x5, local copies, waits for them, and re-layouts, splat(): embedded[:, None, :] * row_kernel[level][None]  16.6 us
    unnamed x51, local copies, waits for them, and re-layouts  13.7 us
    all_to_all x1, starting transfers between devices, on_device(): lax.all_to_all(outgoing, 'band', split_axis=1, concat_axis=1, tiled=True)  13.4 us
    dot_general x4, matrix products, splat(): lax.dot_general(weighted, column_kernel[level], (((1,), (1,)), ((), ())),...  13 us
    all_to_all x1, waiting for transfers between devices, on_device(): lax.all_to_all(outgoing, 'band', split_axis=1, concat_axis=1, tiled=True)  12.5 us
  transfers between devices with their start and end apart: 5, of which 4 were waited for; matrix products, arithmetic and copies ran while one was open for 4% of the time, Pallas kernels for 0%

commit v1 on v0

v1 whole, which is shorter than its diff:
```python
import jax
import jax.numpy as jnp
from jax import lax
from jax.experimental import pallas as pl
from jax.experimental.pallas import tpu as pltpu
from jax.sharding import PartitionSpec as P

MESH = pl.DeviceIdType.MESH
bf16 = jnp.bfloat16
f32 = jnp.float32

root_two_pi = 0.7978845608028654
cubic = 0.044715
half_log2e = 0.8493218002880191

BANDS = 64
REPS = 4
YS, ZS, CORES = 4, 8, 2
CAP = 20
TILE = 16
ROWS = BANDS * TILE
REPORTS = 512
LEVELS = 4
CH = 128
PART = 32
SUB = 3
NLON = 256
LAT = 12.0
CELLS = SUB * NLON
HID = 512
GROWS = 4096


def iota(shape, dim):
    return lax.broadcasted_iota(jnp.int32, shape, dim)


def one_where(cond):
    return jnp.where(cond, 1.0, 0.0).astype(bf16)


def dot(a, b):
    return lax.dot_general(a, b, (((1,), (0,)), ((), ())), preferred_element_type=f32)


def dot_nt(a, b):
    return lax.dot_general(a, b, (((1,), (1,)), ((), ())), preferred_element_type=f32)


def eye(n):
    return one_where(iota((n, n), 0) == iota((n, n), 1))


def row_keys(start, rows):
    row = iota((rows, 1), 0) + start
    band = row >> 4
    ok = row & 15
    key = jnp.where(ok == 15, -1000, (band - 1) * 5 + ok).astype(f32)
    place_band = jnp.where(ok == 15, band, -1000).astype(f32)
    return key, place_band


def report_ranks(route_ref):
    owner = jnp.zeros((1, REPORTS), f32)
    cols = []
    for part in range(4):
        col = route_ref[part * 128 : (part + 1) * 128, :].astype(f32)
        cols.append(col)
        same = iota((128, REPORTS), 0) + part * 128 == iota((128, REPORTS), 1)
        owner = owner + jnp.sum(jnp.where(same, col, 0.0), axis=0, keepdims=True)
    rank = jnp.zeros((1, REPORTS), f32)
    for part in range(4):
        before = iota((128, REPORTS), 0) + part * 128 < iota((128, REPORTS), 1)
        rank = rank + jnp.sum(
            jnp.where((cols[part] == owner) & before, 1.0, 0.0), axis=0, keepdims=True
        )
    return owner, rank


def greet(me, rep):
    barrier = pltpu.get_barrier_semaphore()

    def band_peer(d, carry):
        pl.semaphore_signal(
            barrier, inc=1, device_id=(lax.rem(me + d, BANDS), rep), device_id_type=MESH
        )
        return carry

    lax.fori_loop(1, BANDS, band_peer, 0)
    for d in range(1, REPS):
        pl.semaphore_signal(
            barrier, inc=1, device_id=(me, lax.rem(rep + d, REPS)), device_id_type=MESH
        )
    return barrier


def send_tiles(me, rep, table, landing, send_sem, recv_sem):
    def send(d, carry):
        peer = lax.rem(me + d, BANDS)
        pltpu.make_async_remote_copy(
            src_ref=table.at[pl.ds(pl.multiple_of(peer * TILE, TILE), TILE)],
            dst_ref=landing.at[pl.ds(pl.multiple_of(me * TILE, TILE), TILE)],
            send_sem=send_sem,
            recv_sem=recv_sem,
            device_id=(peer, rep),
            device_id_type=MESH,
        ).start()
        return carry

    lax.fori_loop(1, BANDS, send, 0)


def tiles_done(me, rep, table, landing, send_sem, recv_sem):
    return pltpu.make_async_remote_copy(
        src_ref=table.at[pl.ds(0, ROWS - TILE)],
        dst_ref=landing.at[pl.ds(0, ROWS - TILE)],
        send_sem=send_sem,
        recv_sem=recv_sem,
        device_id=(lax.rem(me + 1, BANDS), rep),
        device_id_type=MESH,
    )


def gather_kernel(emb_ref, route_ref, place_ref, rr_ref, keys_ref, table, ssem, rsem, xs, xr):
    me = lax.axis_index("band")
    rep = lax.axis_index("rep")
    barrier = greet(me, rep)
    owner, rank = report_ranks(route_ref)
    quad = jnp.floor(rank * 0.25)
    within = rank - 4.0 * quad
    key = owner * 5.0 + quad
    third = owner - 3.0 * jnp.floor((owner + 0.5) * (1.0 / 3.0))
    pad = jnp.zeros((6, REPORTS), f32)
    keys_ref[...] = jnp.concatenate([key, within, pad], axis=0)
    emb = emb_ref[...].astype(f32)
    emb_b = jnp.concatenate(
        [jnp.where(within == float(s), emb, 0.0) for s in range(4)], axis=0
    ).astype(bf16)
    lam = iota((128, REPORTS), 0).astype(f32)
    spot = third * 20.0 + rank
    north = place_ref[0:1, :].astype(f32)
    east = place_ref[1:2, :].astype(f32)
    place_b = (
        jnp.where(lam == spot, north, 0.0)
        + jnp.where(lam == spot + 64.0, east, 0.0)
        + jnp.where(lam == third + 60.0, 1.0, 0.0)
    ).astype(bf16)
    for part in range(8):
        row_key, place_band = row_keys(part * 128, 128)
        pick = one_where(row_key == key)
        near = one_where(jnp.abs(place_band - owner) <= 1.0)
        table[part * 128 : (part + 1) * 128, :] = (
            dot_nt(pick, emb_b) + dot_nt(near, place_b)
        ).astype(bf16)
    pl.semaphore_wait(barrier, BANDS - 1 + REPS - 1)
    landing = rr_ref.at[rep]
    send_tiles(me, rep, table, landing, ssem, rsem)
    own = pl.ds(pl.multiple_of(me * TILE, TILE), TILE)
    rr_ref[rep, own, :] = table[own, :]
    done = tiles_done(me, rep, table, landing, ssem, rsem)
    done.wait_recv()
    copies = []
    for d in range(1, REPS):
        copy = pltpu.make_async_remote_copy(
            src_ref=rr_ref.at[rep],
            dst_ref=rr_ref.at[rep],
            send_sem=xs.at[d],
            recv_sem=xr.at[d],
            device_id=(me, lax.rem(rep + d, REPS)),
            device_id_type=MESH,
        )
        copy.start()
        copies.append(copy)
    done.wait_send()
    for copy in copies:
        copy.wait()


def decode_places(t, rep, expand, base_ref, east_ref, valid_ref):
    lane = iota((1, ROWS), 1)
    ok = lane & 15
    o = (ok >= 5).astype(jnp.int32) + (ok >= 10).astype(jnp.int32) + (ok >= 15).astype(jnp.int32)
    k4 = (ok - 5 * o) * 4
    v = lax.rem(t + 2, 3) + o
    third = jnp.where(v >= 3, v - 3, v)
    code = third * 20 + k4
    lam = iota((64, ROWS), 0)
    low = expand[0:64, :]
    high = expand[64:128, :]
    count = jnp.sum(jnp.where(lam == third + 60, low, 0.0), axis=0, keepdims=True)
    offset = (1 - o).astype(f32) * LAT + (rep * SUB).astype(f32) + 0.5
    for s in range(4):
        hit = lam == code + s
        north = jnp.sum(jnp.where(hit, low, 0.0), axis=0, keepdims=True)
        east = jnp.sum(jnp.where(hit, high, 0.0), axis=0, keepdims=True)
        valid = jnp.where((ok < 15) & ((k4 + s).astype(f32) < count), 1.0, 0.0)
        base_ref[s] = jnp.broadcast_to(offset - north * LAT, (16, ROWS))
        valid_ref[s] = jnp.broadcast_to(valid, (16, ROWS))
        east_ref[s] = jnp.broadcast_to(east * float(NLON), (8, ROWS))


def local_kernel(
    rr_ref, scales_ref, w1_ref, b1_ref, w2_ref, cot_ref,
    d_ref, g_ref, bias_ref,
    emb_t, expand, base_ref, east_ref, valid_ref, col_ref, rowf_ref, w_ref, acc_ref,
    feat_ref, w1p_ref, w1t_ref, bcol_ref, hid_ref, pg_ref, sg_ref, tot_ref,
):
    t = lax.axis_index("band")
    rep = lax.axis_index("rep")
    ident = eye(128)
    group = one_where(
        ((iota((128, 128), 0) >> 4) == (iota((128, 128), 1) >> 4)) & ((iota((128, 128), 0) & 15) == 15)
    )
    for q in range(REPS):
        turned = dot_nt(ident, rr_ref[q]).astype(bf16)
        for s in range(4):
            emb_t[s, q * PART : (q + 1) * PART, :] = turned[s * PART : (s + 1) * PART, :]
        if q == 0:
            for b in range(8):
                expand[:, b * 128 : (b + 1) * 128] = dot(turned[:, b * 128 : (b + 1) * 128], group)
    decode_places(t, rep, expand, base_ref, east_ref, valid_ref)
    acc_ref[...] = jnp.zeros_like(acc_ref)

    def splat(it, carry):
        s = it >> 2
        level = it & 3
        reach = scales_ref[level] * LAT
        scale = half_log2e / jnp.full((1, 128), reach, f32)
        scale_wide = jnp.concatenate([scale] * 8, axis=1)
        east = east_ref[s, 0:1, :] * scale_wide
        for c in range(8):
            centre = (iota((32, 128), 0).astype(f32) + (c * 32 + 0.5)) * scale
            for b in range(8):
                gap = centre - east[:, b * 128 : (b + 1) * 128]
                col_ref[it, c * 32 : (c + 1) * 32, b * 128 : (b + 1) * 128] = jnp.exp2(
                    -(gap * gap)
                ).astype(bf16)
        valid = valid_ref[s]
        rows = []
        for i in range(SUB):
            gap = (base_ref[s] + float(i)) * scale_wide
            rows.append((jnp.exp2(-(gap * gap)) * valid).astype(bf16))
        sub = iota((16, ROWS), 0)
        wide = [r.astype(f32) for r in rows]
        mixed = jnp.where(
            sub == 0, wide[0], jnp.where(sub == 1, wide[1], jnp.where(sub == 2, wide[2], 0.0))
        )
        rowf_ref[it] = mixed[0:8, :]
        w_ref[SUB * CH : SUB * CH + 16, :] = mixed.astype(bf16)
        for c in range(8):
            e = emb_t[s, c * 16 : (c + 1) * 16, :]
            for i in range(SUB):
                w_ref[i * CH + c * 16 : i * CH + (c + 1) * 16, :] = e * rows[i]
        acc_ref[level] += dot_nt(w_ref[...], col_ref[it])
        return carry

    lax.fori_loop(0, 16, splat, 0)

    def inverse(level, i):
        return 1.0 / (acc_ref[level, SUB * CH + i : SUB * CH + i + 1, :] + 1.0)

    for level in range(LEVELS):
        for i in range(SUB):
            feat_ref[level * CH : (level + 1) * CH, i * NLON : (i + 1) * NLON] = (
                acc_ref[level, i * CH : (i + 1) * CH, :] * inverse(level, i)
            ).astype(bf16)

    r512 = iota((512, 512), 0)
    c512 = iota((512, 512), 1)
    w1p_ref[...] = dot(one_where(c512 == (r512 & 127) * 4 + (r512 >> 7)), w1_ref[...]).astype(bf16)
    w1t_ref[...] = dot_nt(eye(512), w1p_ref[...]).astype(bf16)
    bcol_ref[...] = jnp.sum(jnp.where(r512 == c512, b1_ref[...], 0.0), axis=1, keepdims=True)

    for i in range(SUB):
        cells = slice(i * NLON, (i + 1) * NLON)
        for h in range(2):
            rows = slice(h * 256, (h + 1) * 256)
            pre = dot(w1t_ref[rows, :], feat_ref[:, cells]) + bcol_ref[rows, :]
            above = dot(w2_ref[rows, :], cot_ref[:, cells])
            square = pre * pre
            tangent = jnp.tanh(root_two_pi * (pre + cubic * square * pre))
            hid_ref[rows, cells] = (0.5 * pre * (1.0 + tangent)).astype(bf16)
            slope = 0.5 * (1.0 + tangent) + 0.5 * pre * (1.0 - tangent * tangent) * root_two_pi * (
                1.0 + 3.0 * cubic * square
            )
            pg_ref[rows, cells] = (above * slope).astype(bf16)

    back = one_where(c512 == (r512 & 3) * 128 + (r512 >> 2))
    for h in range(2):
        rows = slice(h * 256, (h + 1) * 256)
        first = dot(back, dot_nt(feat_ref[...], pg_ref[rows, :]).astype(bf16)).astype(bf16)
        second = dot_nt(hid_ref[...], cot_ref[rows, :]).astype(bf16)
        for c in range(2):
            at = (h * 2 + c) * 1024
            g_ref[at : at + 512, :] = first[:, c * 128 : (c + 1) * 128]
            g_ref[at + 512 : at + 1024, :] = second[:, c * 128 : (c + 1) * 128]
    bias = dot_nt(jnp.ones((16, CELLS), bf16), pg_ref[...])
    bias_ref[...] = jnp.concatenate(
        [bias[0:1, c * 128 : (c + 1) * 128] for c in range(4)] + [jnp.zeros((4, 128), f32)], axis=0
    )

    for i in range(SUB):
        grad = dot(w1p_ref[...], pg_ref[:, i * NLON : (i + 1) * NLON])
        for level in range(LEVELS):
            sg_ref[level, i * CH : (i + 1) * CH, :] = (
                grad[level * CH : (level + 1) * CH, :] * inverse(level, i)
            ).astype(bf16)

    def spread(s, carry):
        tot_ref[...] = jnp.zeros_like(tot_ref)

        def one_level(level, inner):
            it = s * 4 + level
            for n in range(4):
                lanes = slice(n * 256, (n + 1) * 256)
                along = dot(sg_ref[level], col_ref[it, :, lanes])
                total = tot_ref[:, lanes]
                for i in range(SUB):
                    total = total + along[i * CH : (i + 1) * CH, :] * rowf_ref[it, i : i + 1, lanes]
                tot_ref[:, lanes] = total
            return inner

        lax.fori_loop(0, LEVELS, one_level, 0)
        at = pl.ds(pl.multiple_of(s * PART, PART), PART)
        for q in range(REPS):
            d_ref[q, at, :] = tot_ref[q * PART : (q + 1) * PART, :].astype(bf16)
        return carry

    lax.fori_loop(0, 4, spread, 0)


def reduce_kernel(
    d_ref, g_ref, bias_ref, keys_ref,
    eg_ref, full_ref, bout_ref,
    d_in, table, landing, pick_ref, g1, g2, g3, in_c, in_y, in_z, in_x, bc, by, bz, bx,
    ds, dr, ssem, rsem, gs, gr, bs, br, as_, ar,
):
    me = lax.axis_index("band")
    rep = lax.axis_index("rep")
    core = lax.rem(me, CORES)
    z = lax.rem(me // CORES, ZS)
    y = me // (CORES * ZS)
    barrier = greet(me, rep)
    key = keys_ref[0:1, :]
    within = keys_ref[1:2, :]
    pl.semaphore_wait(barrier, BANDS - 1 + REPS - 1)

    def core_peer(d):
        return me + 1 - 2 * core, rep

    def y_peer(d):
        return lax.rem(y + d, YS) * (CORES * ZS) + z * CORES + core, rep

    def z_peer(d):
        return y * (CORES * ZS) + lax.rem(z + d, ZS) * CORES + core, rep

    def x_peer(d):
        return me, lax.rem(rep + d, REPS)

    def start(src, dst, send, recv, device):
        copy = pltpu.make_async_remote_copy(
            src_ref=src, dst_ref=dst, send_sem=send, recv_sem=recv, device_id=device, device_id_type=MESH
        )
        copy.start()
        return copy

    def rows_at(index, size):
        return pl.ds(pl.multiple_of(index * size, size), size)

    def scatter(src, dst, size, n, mine, peer, base):
        return [
            start(
                src.at[rows_at(lax.rem(mine + d, n), size)], dst.at[d - 1],
                gs.at[base + d - 1], gr.at[base + d - 1], peer(d),
            )
            for d in range(1, n)
        ]

    def bias_round(value, slots, n, mine, peer, base):
        slots[mine] = value
        return [
            start(slots.at[mine], slots.at[mine], bs.at[base + d - 1], br.at[base + d - 1], peer(d))
            for d in range(1, n)
        ]

    def bias_sum(slots, n):
        total = slots[0]
        for k in range(1, n):
            total = total + slots[k]
        return total

    def finish(copies):
        for copy in copies:
            copy.wait()

    def spread_out(offset, size, n, peer, base):
        at = pl.ds(pl.multiple_of(offset, size), size)
        return [
            start(full_ref.at[at], full_ref.at[at], as_.at[base + d - 1], ar.at[base + d - 1], peer(d))
            for d in range(1, n)
        ]

    d_copies = [
        start(d_ref.at[lax.rem(rep + d, REPS)], d_in.at[d - 1], ds.at[d - 1], dr.at[d - 1], x_peer(d))
        for d in range(1, REPS)
    ]
    c_copies = scatter(g_ref, in_c, 2048, CORES, core, core_peer, 0)
    c_bias = bias_round(bias_ref[...], bc, CORES, core, core_peer, 0)
    for part in range(8):
        row_key, _ = row_keys(part * 128, 128)
        pick_ref[part * 128 : (part + 1) * 128, :] = one_where(row_key == key)
    finish(c_copies)
    g1[...] = (g_ref[rows_at(core, 2048), :].astype(f32) + in_c[0].astype(f32)).astype(bf16)
    y_copies = scatter(g1, in_y, 512, YS, y, y_peer, 1)
    finish(c_bias)
    y_bias = bias_round(bias_sum(bc, CORES), by, YS, y, y_peer, 1)
    finish(y_copies)
    total = g1[rows_at(y, 512), :].astype(f32)
    for d in range(YS - 1):
        total = total + in_y[d].astype(f32)
    g2[...] = total.astype(bf16)
    z_copies = scatter(g2, in_z, 64, ZS, z, z_peer, 4)
    finish(y_bias)
    z_bias = bias_round(bias_sum(by, YS), bz, ZS, z, z_peer, 4)
    finish(d_copies)
    part = d_ref[rep].astype(f32)
    for d in range(REPS - 1):
        part = part + d_in[d].astype(f32)
    table[...] = jnp.transpose(part).astype(bf16)
    send_tiles(me, rep, table, landing, ssem, rsem)
    own = rows_at(me, TILE)
    landing[own, :] = table[own, :]
    finish(z_copies)
    total = g2[rows_at(z, 64), :].astype(f32)
    for d in range(ZS - 1):
        total = total + in_z[d].astype(f32)
    g3[...] = total.astype(bf16)
    x_copies = scatter(g3, in_x, 16, REPS, rep, x_peer, 11)
    finish(z_bias)
    x_bias = bias_round(bias_sum(bz, ZS), bx, REPS, rep, x_peer, 11)
    finish(x_copies)
    total = g3[rows_at(rep, 16), :].astype(f32)
    for d in range(REPS - 1):
        total = total + in_x[d].astype(f32)
    at_z = core * 2048 + y * 512 + z * 64
    full_ref[pl.ds(pl.multiple_of(at_z + rep * 16, 16), 16), :] = total.astype(bf16)
    copies = spread_out(at_z + rep * 16, 16, REPS, x_peer, 0)
    finish(x_bias)
    bout_ref[...] = bias_sum(bx, REPS)
    finish(copies)
    copies = spread_out(at_z, 64, ZS, z_peer, 3)
    finish(copies)
    copies = spread_out(core * 2048 + y * 512, 512, YS, y_peer, 10)
    tiles_done(me, rep, table, landing, ssem, rsem).wait()
    turned = dot_nt(eye(128), landing[...]).astype(bf16)
    found = dot(turned, pick_ref[...])
    gradient = jnp.zeros((PART, REPORTS), f32)
    for s in range(4):
        gradient = gradient + jnp.where(within == float(s), found[s * PART : (s + 1) * PART, :], 0.0)
    eg_ref[...] = gradient
    finish(copies)
    finish(spread_out(core * 2048, 2048, CORES, core_peer, 13))


def vmem(n):
    return [pl.BlockSpec(memory_space=pltpu.VMEM)] * n


def sds(shape, dtype):
    return jax.ShapeDtypeStruct(shape, dtype)


def on_device(
    embeddings, route, place, scales, first_weight, first_bias, second_weight, out_cotangent
):
    rr, keys = pl.pallas_call(
        gather_kernel,
        out_shape=[sds((REPS, ROWS, 128), bf16), sds((8, REPORTS), f32)],
        in_specs=vmem(3),
        out_specs=vmem(2),
        scratch_shapes=[
            pltpu.VMEM((ROWS, 128), bf16),
            pltpu.SemaphoreType.DMA,
            pltpu.SemaphoreType.DMA,
            pltpu.SemaphoreType.DMA((REPS,)),
            pltpu.SemaphoreType.DMA((REPS,)),
        ],
        compiler_params=pltpu.CompilerParams(
            collective_id=0, has_side_effects=True, vmem_limit_bytes=32 << 20
        ),
    )(embeddings, route, place)
    cotangent = out_cotangent.reshape(out_cotangent.shape[0], CELLS)
    slot, grads, bias = pl.pallas_call(
        local_kernel,
        out_shape=[
            sds((REPS, 128, ROWS), bf16),
            sds((GROWS, 128), bf16),
            sds((8, 128), f32),
        ],
        in_specs=vmem(1) + [pl.BlockSpec(memory_space=pltpu.SMEM)] + vmem(4),
        out_specs=vmem(3),
        scratch_shapes=[
            pltpu.VMEM((4, CH, ROWS), bf16),
            pltpu.VMEM((128, ROWS), f32),
            pltpu.VMEM((4, 16, ROWS), f32),
            pltpu.VMEM((4, 8, ROWS), f32),
            pltpu.VMEM((4, 16, ROWS), f32),
            pltpu.VMEM((16, NLON, ROWS), bf16),
            pltpu.VMEM((16, 8, ROWS), f32),
            pltpu.VMEM((SUB * CH + 16, ROWS), bf16),
            pltpu.VMEM((LEVELS, SUB * CH + 16, NLON), f32),
            pltpu.VMEM((512, CELLS), bf16),
            pltpu.VMEM((512, HID), bf16),
            pltpu.VMEM((HID, 512), bf16),
            pltpu.VMEM((HID, 1), f32),
            pltpu.VMEM((HID, CELLS), bf16),
            pltpu.VMEM((HID, CELLS), bf16),
            pltpu.VMEM((LEVELS, SUB * CH, NLON), bf16),
            pltpu.VMEM((CH, ROWS), f32),
        ],
        compiler_params=pltpu.CompilerParams(vmem_limit_bytes=52 << 20),
    )(rr, scales, first_weight, first_bias.reshape(1, HID), second_weight, cotangent)
    dma = pltpu.SemaphoreType.DMA
    gradient, full, bias_total = pl.pallas_call(
        reduce_kernel,
        out_shape=[
            sds((PART, REPORTS), f32),
            sds((GROWS, 128), bf16),
            sds((8, 128), f32),
        ],
        in_specs=vmem(4),
        out_specs=vmem(3),
        scratch_shapes=[
            pltpu.VMEM((REPS - 1, 128, ROWS), bf16),
            pltpu.VMEM((ROWS, 128), bf16),
            pltpu.VMEM((ROWS, 128), bf16),
            pltpu.VMEM((ROWS, REPORTS), bf16),
            pltpu.VMEM((2048, 128), bf16),
            pltpu.VMEM((512, 128), bf16),
            pltpu.VMEM((64, 128), bf16),
            pltpu.VMEM((1, 2048, 128), bf16),
            pltpu.VMEM((3, 512, 128), bf16),
            pltpu.VMEM((7, 64, 128), bf16),
            pltpu.VMEM((3, 16, 128), bf16),
            pltpu.VMEM((CORES, 8, 128), f32),
            pltpu.VMEM((YS, 8, 128), f32),
            pltpu.VMEM((ZS, 8, 128), f32),
            pltpu.VMEM((REPS, 8, 128), f32),
            dma((REPS - 1,)), dma((REPS - 1,)),
            dma, dma,
            dma((14,)), dma((14,)),
            dma((14,)), dma((14,)),
            dma((14,)), dma((14,)),
        ],
        compiler_params=pltpu.CompilerParams(
            collective_id=1, has_side_effects=True, vmem_limit_bytes=32 << 20
        ),
    )(slot, grads, bias, keys)
    both = full.reshape(4, 2, 512, 128).transpose(1, 2, 0, 3).reshape(2, 512, 512).astype(f32)
    return (gradient, both[0], bias_total[0:4].reshape(HID), both[1])


def solution(mesh):
    return jax.shard_map(
        on_device,
        mesh=mesh,
        in_specs=(
            P("rep", "band"),
            P("band", None),
            P(None, "band"),
            P(),
            P(),
            P(),
            P(),
            P(None, ("band", "rep"), None),
        ),
        out_specs=(P("rep", "band"), P(), P(), P()),
        check_vma=False,
    )
```

time: 451 us -> 114 us (0.25); the launches traced: 443 us -> 113 us
  waiting for transfers between devices: 206 us -> 0 us
  Pallas kernels: 0 us -> 102 us
  blocking collectives: 76.4 us -> 0 us
  local copies, waits for them, and re-layouts: 61.9 us -> 10.2 us
  matrix products: 33 us -> 0 us
  starting transfers between devices: 29.4 us -> 0 us
  other arithmetic: 21.3 us -> 0.14 us
  between operations: 14.9 us -> 0.77 us
    psum x1 -> x0, waiting for transfers between devices: 178 us -> none  [on_device(): totals = lax.psum((first_sum, second_sum, bias_sum), ('band', 'rep'))]
    pallas_call x0 -> x3, Pallas kernels: none -> 102 us  [the longest x1 44.5 us: on_device(): pl.pallas_call(reduce_kernel, out_shape=[sds((PART, REPORTS), f32), sds((...]
    psum x1 -> x0, blocking collectives: 76.4 us -> none  [on_device(): totals = lax.psum((first_sum, second_sum, bias_sum), ('band', 'rep'))]
    dot_general x17 -> x0, matrix products: 33 us -> none  [the longest x4 13 us: splat(): lax.dot_general(weighted, column_kernel[level], (((1,), (1,)), ((), ())),...]
    all_to_all x4 -> x0, starting transfers between devices: 29.3 us -> none  [the longest x1 13.4 us: on_device(): lax.all_to_all(outgoing, 'band', split_axis=1, concat_axis=1, tiled=True)]
    all_to_all x4 -> x0, waiting for transfers between devices: 28.3 us -> none  [the longest x1 12.5 us: on_device(): lax.all_to_all(outgoing, 'band', split_axis=1, concat_axis=1, tiled=True)]
    mul x8 -> x0, local copies, waits for them, and re-layouts: 16.8 us -> none  [the longest x5 16.6 us: splat(): embedded[:, None, :] * row_kernel[level][None]]
    mul x4 -> x0, other arithmetic: 8.15 us -> none  [the longest x1 6.77 us: splat(): embedded[:, None, :] * row_kernel[level][None]]
  transfers between devices with their start and end apart: 5 -> 0, of which waited for: 4 -> 0; matrix products, arithmetic and copies ran while one was open for 4% -> 0% of each run, Pallas kernels for 0% -> 0%
where the time goes in v1:
time: 114 us; the launch traced here: 113 us
  Pallas kernels  102 us (89%)
  local copies, waits for them, and re-layouts  10.2 us (9%)
    pallas_call x1, Pallas kernels, on_device(): pl.pallas_call(reduce_kernel, out_shape=[sds((PART, REPORTS), f32), sds((...  44.5 us
    pallas_call x1, Pallas kernels, on_device(): pl.pallas_call(gather_kernel, out_shape=[sds((REPS, ROWS, 128), bf16), sd...  34.2 us
    pallas_call x1, Pallas kernels, on_device(): pl.pallas_call(local_kernel, out_shape=[sds((REPS, 128, ROWS), bf16), sds...  23.6 us
    unnamed x21, local copies, waits for them, and re-layouts  6.38 us

profile of v1, /device:TPU:1, one launch (start us, length us, event | category | flops | bytes accessed | tf_op | source)
XLA Modules:
  0.0 113.4 jit_solution(17777795544293730101)
XLA Ops:
  0.6 0.0 copy-start.4
  0.6 0.0 copy-start.7
  0.7 0.0 copy-start.3
  0.7 0.0 copy-start.8
  0.7 0.0 copy-start.6
  0.7 0.9 copy.16.route_ref
  1.6 1.4 %copy.17 = bf16[512,3,256]{0,2,1:T(8,128)(2,1)S(1)} copy(bf16[512,3,256]{2,0,1:T(8,128)(2,1)} %param.15) | data formatting | bytes 1572864 | tf_op args[7]
  3.0 0.3 copy.18.cot_ref
  3.3 34.2 %shard_map.111 = (bf16[4,1024,128]{2,1,0:T(8,128)(2,1)S(1)}, f32[8,512]{1,0:T(8,128)S(1)}) custom-call(bf16[32,512]{1,0:T(8,128)(2,1)S(1)} %copy-done.5, s32[512,1]{1,0:T(8,128)S(1)} %copy.16.route_ref, bf16[2,512]{1,0:T(2,128)(2,1)S(1)} %copy-done.6), custom_call_target="tpu_custom_call" | custom-call | tf_op jit(solution)/shard_map/pallas_call | solution.py:476
  37.5 0.0 copy-start.2
  37.5 1.0 copy-done.2
  38.5 0.0 copy-done.7
  38.5 0.0 copy-done.8
  38.5 23.6 %shard_map.112 = (bf16[4,128,1024]{2,1,0:T(8,128)(2,1)}, bf16[4096,128]{1,0:T(8,128)(2,1)}, f32[8,128]{1,0:T(8,128)S(1)}) custom-call(bf16[4,1024,128]{2,1,0:T(8,128)(2,1)} %copy-done.2, f32[4]{0:T(128)S(1)} %copy-done.8, bf16[512,512]{1,0:T(8,128)(2,1)S(1)} %copy-done.3, f32[1,512]{1,0:T(1,128)S(1)} %bitcast.17, bf16[512,512]{1,0:T(8,128)(2,1)S(1)} %copy-done.4, ...), custom_call_target="tpu_custom_call" | custom-call | tf_op jit(solution)/shard_map/pallas_call | solution.py:493
  62.1 1.2 %copy-done = bf16[4,128,1024]{2,1,0:T(8,128)(2,1)S(1)} copy-done((bf16[4,128,1024]{2,1,0:T(8,128)(2,1)S(1)}, bf16[4,128,1024]{2,1,0:T(8,128)(2,1)}, u32[]{:S(2)}) %copy-start) | copy-done | bytes 1048600
  63.3 1.2 %copy-done.1 = bf16[4096,128]{1,0:T(8,128)(2,1)S(1)} copy-done((bf16[4096,128]{1,0:T(8,128)(2,1)S(1)}, bf16[4096,128]{1,0:T(8,128)(2,1)}, u32[]{:S(2)}) %copy-start.1) | copy-done | bytes 1048600
  64.5 44.5 %shard_map.113 = (f32[32,512]{1,0:T(8,128)S(1)}, bf16[4096,128]{1,0:T(8,128)(2,1)S(1)}, f32[8,128]{1,0:T(8,128)S(1)}) custom-call(bf16[4,128,1024]{2,1,0:T(8,128)(2,1)S(1)} %copy-done, bf16[4096,128]{1,0:T(8,128)(2,1)S(1)} %copy-done.1, f32[8,128]{1,0:T(8,128)S(1)} %get-tuple-element.15.bias_ref, f32[8,512]{1,0:T(8,128)S(1)} %get-tuple-element.16.keys_ref), custom_call_target="tpu_custom_call" | custom-call | tf_op jit(solution)/shard_map/pallas_call | solution.py:524
  109.1 0.6 slice_bitcast_fusion
  109.7 0.1 convert_bitcast_fusion
  109.8 0.1 fusion
  109.9 0.7 copy.20
  110.6 0.7 copy.19
  111.3 1.5 %copy_bitcast_fusion = (f32[512,512]{1,0:T(8,128)}, f32[512,512]{1,0:T(8,128)}) fusion(f32[64,8,4,128]{3,2,1,0:T(4,128)S(1)} %bitcast.18, f32[64,8,4,128]{3,2,1,0:T(4,128)S(1)} %bitcast.19), kind=kLoop, calls=%fused_computation.1 | loop fusion | bytes 4194304 | tf_op jit(solution)/shard_map/squeeze | solution.py:560
  112.8 0.6 copy.26
  (7 shorter events, 0.0 us)
Async XLA Ops:
  0.6 37.9 %copy-start.4 = (bf16[512,512]{1,0:T(8,128)(2,1)S(1)}, bf16[512,512]{1,0:T(8,128)(2,1)}, u32[]{:S(2)}) copy-start(bf16[512,512]{1,0:T(8,128)(2,1)} %w2_ref.1) | copy-start | bytes 1572868
  0.6 37.9 %copy-start.7 = (f32[512]{0:T(512)S(1)}, f32[512]{0:T(512)}, u32[]{:S(2)}) copy-start(f32[512]{0:T(512)} %param.13) | copy-start | bytes 6148
  0.7 37.8 %copy-start.3 = (bf16[512,512]{1,0:T(8,128)(2,1)S(1)}, bf16[512,512]{1,0:T(8,128)(2,1)}, u32[]{:S(2)}) copy-start(bf16[512,512]{1,0:T(8,128)(2,1)} %w1_ref.1) | copy-start | bytes 1572868
  0.7 37.8 %copy-start.8 = (f32[4]{0:T(128)S(1)}, f32[4]{0:T(128)}, u32[]{:S(2)}) copy-start(f32[4]{0:T(128)} %scales_ref.1) | copy-start | bytes 52
  0.7 2.6 %copy-start.6 = (bf16[2,512]{1,0:T(2,128)(2,1)S(1)}, bf16[2,512]{1,0:T(2,128)(2,1)}, u32[]{:S(2)}) copy-start(bf16[2,512]{1,0:T(2,128)(2,1)} %place_ref.1) | copy-start | bytes 6148
  0.7 2.6 %copy-start.5 = (bf16[32,512]{1,0:T(8,128)(2,1)S(1)}, bf16[32,512]{1,0:T(8,128)(2,1)}, u32[]{:S(2)}) copy-start(bf16[32,512]{1,0:T(8,128)(2,1)} %emb_ref.1) | copy-start | bytes 98308
  37.5 1.0 copy-start.2
  62.1 1.2 %copy-start = (bf16[4,128,1024]{2,1,0:T(8,128)(2,1)S(1)}, bf16[4,128,1024]{2,1,0:T(8,128)(2,1)}, u32[]{:S(2)}) copy-start(bf16[4,128,1024]{2,1,0:T(8,128)(2,1)} %get-tuple-element.13.d_ref) | copy-start | bytes 3145732
  63.3 1.2 %copy-start.1 = (bf16[4096,128]{1,0:T(8,128)(2,1)S(1)}, bf16[4096,128]{1,0:T(8,128)(2,1)}, u32[]{:S(2)}) copy-start(bf16[4096,128]{1,0:T(8,128)(2,1)} %get-tuple-element.14.g_ref) | copy-start | bytes 3145732

commit v2 on v1

v2 whole, which is shorter than its diff:
```python
import jax
import jax.numpy as jnp
from jax import lax
from jax.experimental import pallas as pl
from jax.experimental.pallas import tpu as pltpu
from jax.sharding import PartitionSpec as P

MESH = pl.DeviceIdType.MESH
bf16 = jnp.bfloat16
f32 = jnp.float32

root_two_pi = 0.7978845608028654
cubic = 0.044715
half_log2e = 0.8493218002880191

BANDS = 64
REPS = 4
YS, ZS, CORES = 4, 8, 2
CAP = 20
TILE = 16
ROWS = BANDS * TILE
REPORTS = 512
LEVELS = 4
CH = 128
PART = 32
SUB = 3
NLON = 256
LAT = 12.0
CELLS = SUB * NLON
HID = 512
GROWS = 4096


def iota(shape, dim):
    return lax.broadcasted_iota(jnp.int32, shape, dim)


def one_where(cond):
    return jnp.where(cond, 1.0, 0.0).astype(bf16)


def dot(a, b):
    return lax.dot_general(a, b, (((1,), (0,)), ((), ())), preferred_element_type=f32)


def dot_nt(a, b):
    return lax.dot_general(a, b, (((1,), (1,)), ((), ())), preferred_element_type=f32)


def eye(n):
    return one_where(iota((n, n), 0) == iota((n, n), 1))


def row_keys(start, rows):
    row = iota((rows, 1), 0) + start
    band = row >> 4
    ok = row & 15
    key = jnp.where(ok == 15, -1000, (band - 1) * 5 + ok).astype(f32)
    place_band = jnp.where(ok == 15, band, -1000).astype(f32)
    return key, place_band


def report_ranks(route_ref):
    owner = route_ref[...].astype(f32)
    rank = jnp.zeros((1, REPORTS), f32)
    for part in range(4):
        mine = iota((128, REPORTS), 0) + part * 128
        lane = iota((128, REPORTS), 1)
        col = jnp.sum(jnp.where(mine == lane, owner, 0.0), axis=1, keepdims=True)
        rank = rank + jnp.sum(
            jnp.where((col == owner) & (mine < lane), 1.0, 0.0), axis=0, keepdims=True
        )
    return owner, rank


def greet(me, rep):
    barrier = pltpu.get_barrier_semaphore()

    def band_peer(d, carry):
        pl.semaphore_signal(
            barrier, inc=1, device_id=(lax.rem(me + d, BANDS), rep), device_id_type=MESH
        )
        return carry

    lax.fori_loop(1, BANDS, band_peer, 0)
    for d in range(1, REPS):
        pl.semaphore_signal(
            barrier, inc=1, device_id=(me, lax.rem(rep + d, REPS)), device_id_type=MESH
        )
    return barrier


def send_tiles(me, rep, table, landing, send_sem, recv_sem):
    def send(d, carry):
        peer = lax.rem(me + d, BANDS)
        pltpu.make_async_remote_copy(
            src_ref=table.at[pl.ds(pl.multiple_of(peer * TILE, TILE), TILE)],
            dst_ref=landing.at[pl.ds(pl.multiple_of(me * TILE, TILE), TILE)],
            send_sem=send_sem,
            recv_sem=recv_sem,
            device_id=(peer, rep),
            device_id_type=MESH,
        ).start()
        return carry

    lax.fori_loop(1, BANDS, send, 0)


def tiles_done(me, rep, table, landing, send_sem, recv_sem):
    return pltpu.make_async_remote_copy(
        src_ref=table.at[pl.ds(0, ROWS - TILE)],
        dst_ref=landing.at[pl.ds(0, ROWS - TILE)],
        send_sem=send_sem,
        recv_sem=recv_sem,
        device_id=(lax.rem(me + 1, BANDS), rep),
        device_id_type=MESH,
    )


def decode_places(t, rep, expand, base_ref, east_ref, valid_ref):
    lane = iota((1, ROWS), 1)
    ok = lane & 15
    o = (ok >= 5).astype(jnp.int32) + (ok >= 10).astype(jnp.int32) + (ok >= 15).astype(jnp.int32)
    k4 = (ok - 5 * o) * 4
    v = lax.rem(t + 2, 3) + o
    third = jnp.where(v >= 3, v - 3, v)
    code = third * 20 + k4
    lam = iota((64, ROWS), 0)
    low = expand[0:64, :]
    high = expand[64:128, :]
    count = jnp.sum(jnp.where(lam == third + 60, low, 0.0), axis=0, keepdims=True)
    offset = (1 - o).astype(f32) * LAT + (rep * SUB).astype(f32) + 0.5
    for s in range(4):
        hit = lam == code + s
        north = jnp.sum(jnp.where(hit, low, 0.0), axis=0, keepdims=True)
        east = jnp.sum(jnp.where(hit, high, 0.0), axis=0, keepdims=True)
        valid = jnp.where((ok < 15) & ((k4 + s).astype(f32) < count), 1.0, 0.0)
        base_ref[s] = jnp.broadcast_to(offset - north * LAT, (16, ROWS))
        valid_ref[s] = jnp.broadcast_to(valid, (16, ROWS))
        east_ref[s] = jnp.broadcast_to(east * float(NLON), (8, ROWS))


def build_table(emb_ref, place_ref, owner, rank, pick_ref, table):
    quad = jnp.floor(rank * 0.25)
    within = rank - 4.0 * quad
    key = owner * 5.0 + quad
    third = owner - 3.0 * jnp.floor((owner + 0.5) * (1.0 / 3.0))
    emb = emb_ref[...].astype(f32)
    emb_b = jnp.concatenate(
        [jnp.where(within == float(s), emb, 0.0) for s in range(4)], axis=0
    ).astype(bf16)
    lam = iota((128, REPORTS), 0).astype(f32)
    spot = third * 20.0 + rank
    north = place_ref[0:1, :].astype(f32)
    east = place_ref[1:2, :].astype(f32)
    place_b = (
        jnp.where(lam == spot, north, 0.0)
        + jnp.where(lam == spot + 64.0, east, 0.0)
        + jnp.where(lam == third + 60.0, 1.0, 0.0)
    ).astype(bf16)
    for part in range(8):
        rows = slice(part * 128, (part + 1) * 128)
        row_key, place_band = row_keys(part * 128, 128)
        pick = one_where(row_key == key)
        pick_ref[rows, :] = pick
        near = one_where(jnp.abs(place_band - owner) <= 1.0)
        table[rows, :] = (dot_nt(pick, emb_b) + dot_nt(near, place_b)).astype(bf16)
    return within


def kernels(it, scales_ref, base_ref, east_ref, valid_ref, col_ref, rk_ref, mix_ref, rowf_ref):
    s = it >> 2
    reach = scales_ref[it & 3] * LAT
    scale = half_log2e / jnp.full((1, 128), reach, f32)
    scale_wide = jnp.concatenate([scale] * 8, axis=1)
    east = east_ref[s, 0:1, :] * scale_wide
    for c in range(8):
        centre = (iota((32, 128), 0).astype(f32) + (c * 32 + 0.5)) * scale
        for b in range(8):
            gap = centre - east[:, b * 128 : (b + 1) * 128]
            col_ref[it, c * 32 : (c + 1) * 32, b * 128 : (b + 1) * 128] = jnp.exp2(
                -(gap * gap)
            ).astype(bf16)
    valid = valid_ref[s]
    wide = []
    for i in range(SUB):
        gap = (base_ref[s] + float(i)) * scale_wide
        row = (jnp.exp2(-(gap * gap)) * valid).astype(bf16)
        rk_ref[it, i] = row
        wide.append(row.astype(f32))
    sub = iota((16, ROWS), 0)
    mixed = jnp.where(
        sub == 0, wide[0], jnp.where(sub == 1, wide[1], jnp.where(sub == 2, wide[2], 0.0))
    )
    rowf_ref[it] = mixed[0:8, :]
    mix_ref[it] = mixed.astype(bf16)


def grid_kernel(
    emb_ref, route_ref, place_ref, scales_ref, w1_hbm, b1_ref, w2_hbm, cot_hbm,
    eg_ref, grads_ref, bout_ref,
    table, rr_ref, pick_ref, w1_ref, w2_ref, cot_ref,
    emb_t, expand, base_ref, east_ref, valid_ref, col_ref, rk_ref, mix_ref, rowf_ref, w_ref, acc_ref,
    feat_ref, w1p_ref, w1t_ref, bcol_ref, hid_ref, pg_ref, sg_ref,
    d_out, d_in, table2, landing, g0, g1, g2, g3, in_c, in_y, in_z, in_x, full_ref, bc, by, bz, bx,
    loads, ssem, rsem, ssem2, rsem2, xs, xr, ds, dr, gs, gr, bs, br, as_, ar,
):
    me = lax.axis_index("band")
    rep = lax.axis_index("rep")
    core = lax.rem(me, CORES)
    z = lax.rem(me // CORES, ZS)
    y = me // (CORES * ZS)

    def core_peer(d):
        return me + 1 - 2 * core, rep

    def y_peer(d):
        return lax.rem(y + d, YS) * (CORES * ZS) + z * CORES + core, rep

    def z_peer(d):
        return y * (CORES * ZS) + lax.rem(z + d, ZS) * CORES + core, rep

    def x_peer(d):
        return me, lax.rem(rep + d, REPS)

    def start(src, dst, send, recv, device):
        copy = pltpu.make_async_remote_copy(
            src_ref=src, dst_ref=dst, send_sem=send, recv_sem=recv, device_id=device, device_id_type=MESH
        )
        copy.start()
        return copy

    def rows_at(index, size):
        return pl.ds(pl.multiple_of(index * size, size), size)

    def scatter(src, dst, size, n, mine, peer, base):
        return [
            start(
                src.at[rows_at(lax.rem(mine + d, n), size)], dst.at[d - 1],
                gs.at[base + d - 1], gr.at[base + d - 1], peer(d),
            )
            for d in range(1, n)
        ]

    def bias_round(value, slots, n, mine, peer, base):
        slots[mine] = value
        return [
            start(slots.at[mine], slots.at[mine], bs.at[base + d - 1], br.at[base + d - 1], peer(d))
            for d in range(1, n)
        ]

    def bias_sum(slots, n):
        total = slots[0]
        for k in range(1, n):
            total = total + slots[k]
        return total

    def finish(copies):
        for copy in copies:
            copy.wait()

    def spread_out(offset, size, n, peer, base):
        at = pl.ds(pl.multiple_of(offset, size), size)
        return [
            start(full_ref.at[at], full_ref.at[at], as_.at[base + d - 1], ar.at[base + d - 1], peer(d))
            for d in range(1, n)
        ]

    barrier = greet(me, rep)
    held = []
    for k, (src, dst) in enumerate(((w1_hbm, w1_ref), (w2_hbm, w2_ref), (cot_hbm, cot_ref))):
        copy = pltpu.make_async_copy(src, dst, loads.at[k])
        copy.start()
        held.append(copy)

    owner, rank = report_ranks(route_ref)
    within = build_table(emb_ref, place_ref, owner, rank, pick_ref, table)
    pl.semaphore_wait(barrier, BANDS - 1 + REPS - 1)
    mine = rr_ref.at[rep]
    send_tiles(me, rep, table, mine, ssem, rsem)
    own = rows_at(me, TILE)
    rr_ref[rep, own, :] = table[own, :]

    finish(held)
    r512 = iota((512, 512), 0)
    c512 = iota((512, 512), 1)
    w1p_ref[...] = dot(one_where(c512 == (r512 & 127) * 4 + (r512 >> 7)), w1_ref[...]).astype(bf16)
    w1t_ref[...] = dot_nt(eye(512), w1p_ref[...]).astype(bf16)
    bcol_ref[...] = jnp.sum(jnp.where(r512 == c512, b1_ref[...], 0.0), axis=1, keepdims=True)

    done = tiles_done(me, rep, table, mine, ssem, rsem)
    done.wait_recv()
    x_copies = []
    for half in range(2):
        rows = pl.ds(half * 512, 512)
        x_copies.append(
            [
                start(
                    rr_ref.at[rep, rows], rr_ref.at[rep, rows],
                    xs.at[half * 3 + d - 1], xr.at[half * 3 + d - 1], x_peer(d),
                )
                for d in range(1, REPS)
            ]
        )

    ident = eye(128)
    group = one_where(
        ((iota((128, 128), 0) >> 4) == (iota((128, 128), 1) >> 4)) & ((iota((128, 128), 0) & 15) == 15)
    )
    turned = dot_nt(ident, rr_ref[rep]).astype(bf16)
    for b in range(8):
        expand[:, b * 128 : (b + 1) * 128] = dot(turned[:, b * 128 : (b + 1) * 128], group)
    decode_places(me, rep, expand, base_ref, east_ref, valid_ref)
    acc_ref[...] = jnp.zeros_like(acc_ref)

    def make(it, carry):
        kernels(it, scales_ref, base_ref, east_ref, valid_ref, col_ref, rk_ref, mix_ref, rowf_ref)
        return carry

    lax.fori_loop(0, 16, make, 0)

    for half in range(2):
        lanes = slice(half * 512, (half + 1) * 512)
        finish(x_copies[half])
        for q in range(REPS):
            turned = dot_nt(ident, rr_ref[q, lanes, :]).astype(bf16)
            for s in range(4):
                emb_t[s, q * PART : (q + 1) * PART, lanes] = turned[s * PART : (s + 1) * PART, :]

        def splat(it, carry):
            s = it >> 2
            level = it & 3
            rows = [rk_ref[it, i, :, lanes] for i in range(SUB)]
            w_ref[SUB * CH : SUB * CH + 16, lanes] = mix_ref[it, :, lanes]
            for c in range(8):
                e = emb_t[s, c * 16 : (c + 1) * 16, lanes]
                for i in range(SUB):
                    w_ref[i * CH + c * 16 : i * CH + (c + 1) * 16, lanes] = e * rows[i]
            acc_ref[level] += dot_nt(w_ref[:, lanes], col_ref[it, :, lanes])
            return carry

        lax.fori_loop(0, 16, splat, 0)
    done.wait_send()

    def inverse(level, i):
        return 1.0 / (acc_ref[level, SUB * CH + i : SUB * CH + i + 1, :] + 1.0)

    for level in range(LEVELS):
        for i in range(SUB):
            feat_ref[level * CH : (level + 1) * CH, i * NLON : (i + 1) * NLON] = (
                acc_ref[level, i * CH : (i + 1) * CH, :] * inverse(level, i)
            ).astype(bf16)

    for i in range(SUB):
        cells = slice(i * NLON, (i + 1) * NLON)
        for h in range(2):
            rows = slice(h * 256, (h + 1) * 256)
            pre = dot(w1t_ref[rows, :], feat_ref[:, cells]) + bcol_ref[rows, :]
            above = dot(w2_ref[rows, :], cot_ref[i])
            square = pre * pre
            tangent = jnp.tanh(root_two_pi * (pre + cubic * square * pre))
            hid_ref[rows, cells] = (0.5 * pre * (1.0 + tangent)).astype(bf16)
            slope = 0.5 * (1.0 + tangent) + 0.5 * pre * (1.0 - tangent * tangent) * root_two_pi * (
                1.0 + 3.0 * cubic * square
            )
            pg_ref[rows, cells] = (above * slope).astype(bf16)

    back = one_where(c512 == (r512 & 3) * 128 + (r512 >> 2))
    for h in range(2):
        rows = slice(h * 256, (h + 1) * 256)
        first = dot(back, dot_nt(feat_ref[...], pg_ref[rows, :]).astype(bf16)).astype(bf16)
        second = dot_nt(hid_ref[:, 0:NLON], cot_ref[0, rows, :])
        for i in range(1, SUB):
            second = second + dot_nt(hid_ref[:, i * NLON : (i + 1) * NLON], cot_ref[i, rows, :])
        second = second.astype(bf16)
        for c in range(2):
            at = (h * 2 + c) * 1024
            g0[at : at + 512, :] = first[:, c * 128 : (c + 1) * 128]
            g0[at + 512 : at + 1024, :] = second[:, c * 128 : (c + 1) * 128]
    bias = dot_nt(jnp.ones((16, CELLS), bf16), pg_ref[...])
    bias_tile = jnp.concatenate(
        [bias[0:1, c * 128 : (c + 1) * 128] for c in range(4)] + [jnp.zeros((4, 128), f32)], axis=0
    )
    c_copies = scatter(g0, in_c, 2048, CORES, core, core_peer, 0)
    c_bias = bias_round(bias_tile, bc, CORES, core, core_peer, 0)

    for i in range(SUB):
        grad = dot(w1p_ref[...], pg_ref[:, i * NLON : (i + 1) * NLON])
        for level in range(LEVELS):
            sg_ref[level, i * CH : (i + 1) * CH, :] = (
                grad[level * CH : (level + 1) * CH, :] * inverse(level, i)
            ).astype(bf16)

    def spread(n):
        lanes = slice(n * 256, (n + 1) * 256)

        def one_group(s, carry):
            total = None
            for level in range(LEVELS):
                it = s * 4 + level
                along = dot(sg_ref[level], col_ref[it, :, lanes])
                for i in range(SUB):
                    term = along[i * CH : (i + 1) * CH, :] * rowf_ref[it, i : i + 1, lanes]
                    total = term if total is None else total + term
            for q in range(REPS):
                d_out[n, q, rows_at(s, PART), :] = total[q * PART : (q + 1) * PART, :].astype(bf16)
            return carry

        lax.fori_loop(0, 4, one_group, 0)
        return [
            start(
                d_out.at[n, lax.rem(rep + d, REPS)], d_in.at[n, d - 1],
                ds.at[n * 3 + d - 1], dr.at[n * 3 + d - 1], x_peer(d),
            )
            for d in range(1, REPS)
        ]

    def to_feeds(n, copies):
        finish(copies)
        total = d_out[n, rep].astype(f32)
        for d in range(REPS - 1):
            total = total + d_in[n, d].astype(f32)
        table2[n * 256 : (n + 1) * 256, :] = jnp.transpose(total).astype(bf16)

        def send(j, carry):
            peer = n * 16 + lax.rem(j + me, 16)

            @pl.when(peer != me)
            def _():
                pltpu.make_async_remote_copy(
                    src_ref=table2.at[rows_at(peer, TILE)],
                    dst_ref=landing.at[rows_at(me, TILE)],
                    send_sem=ssem2,
                    recv_sem=rsem2,
                    device_id=(peer, rep),
                    device_id_type=MESH,
                ).start()

            return carry

        lax.fori_loop(0, 16, send, 0)

    d0 = spread(0)
    finish(c_copies)
    g1[...] = (g0[rows_at(core, 2048), :].astype(f32) + in_c[0].astype(f32)).astype(bf16)
    y_copies = scatter(g1, in_y, 512, YS, y, y_peer, 1)
    finish(c_bias)
    y_bias = bias_round(bias_sum(bc, CORES), by, YS, y, y_peer, 1)
    d1 = spread(1)
    d2 = spread(2)
    to_feeds(0, d0)
    finish(y_copies)
    total = g1[rows_at(y, 512), :].astype(f32)
    for d in range(YS - 1):
        total = total + in_y[d].astype(f32)
    g2[...] = total.astype(bf16)
    z_copies = scatter(g2, in_z, 64, ZS, z, z_peer, 4)
    finish(y_bias)
    z_bias = bias_round(bias_sum(by, YS), bz, ZS, z, z_peer, 4)
    d3 = spread(3)
    to_feeds(1, d1)
    finish(z_copies)
    total = g2[rows_at(z, 64), :].astype(f32)
    for d in range(ZS - 1):
        total = total + in_z[d].astype(f32)
    g3[...] = total.astype(bf16)
    x_copies = scatter(g3, in_x, 16, REPS, rep, x_peer, 11)
    finish(z_bias)
    x_bias = bias_round(bias_sum(bz, ZS), bx, REPS, rep, x_peer, 11)
    to_feeds(2, d2)
    finish(x_copies)
    total = g3[rows_at(rep, 16), :].astype(f32)
    for d in range(REPS - 1):
        total = total + in_x[d].astype(f32)
    at_z = core * 2048 + y * 512 + z * 64
    full_ref[pl.ds(pl.multiple_of(at_z + rep * 16, 16), 16), :] = total.astype(bf16)
    copies = spread_out(at_z + rep * 16, 16, REPS, x_peer, 0)
    finish(x_bias)
    bias_total = bias_sum(bx, REPS)
    for c in range(4):
        bout_ref[:, c * 128 : (c + 1) * 128] = bias_total[c : c + 1, :]
    finish(copies)
    copies = spread_out(at_z, 64, ZS, z_peer, 3)
    to_feeds(3, d3)
    landing[own, :] = table2[own, :]
    finish(copies)
    copies = spread_out(core * 2048 + y * 512, 512, YS, y_peer, 10)
    tiles_done(me, rep, table2, landing, ssem2, rsem2).wait()
    turned = dot_nt(ident, landing[...]).astype(bf16)
    found = dot(turned, pick_ref[...])
    gradient = jnp.zeros((PART, REPORTS), f32)
    for s in range(4):
        gradient = gradient + jnp.where(within == float(s), found[s * PART : (s + 1) * PART, :], 0.0)
    eg_ref[...] = gradient
    finish(copies)
    finish(spread_out(core * 2048, 2048, CORES, core_peer, 13))
    for c in range(4):
        grads_ref[:, c * 128 : (c + 1) * 128] = full_ref[c * 1024 : (c + 1) * 1024, :]


def sds(shape, dtype):
    return jax.ShapeDtypeStruct(shape, dtype)


def on_device(
    embeddings, route, place, scales, first_weight, first_bias, second_weight, out_cotangent
):
    dma = pltpu.SemaphoreType.DMA
    vm = pltpu.VMEM
    in_vmem = pl.BlockSpec(memory_space=pltpu.VMEM)
    anywhere = pl.BlockSpec(memory_space=pl.ANY)
    gradient, grads, bias = pl.pallas_call(
        grid_kernel,
        out_shape=[sds((PART, REPORTS), f32), sds((1024, 512), bf16), sds((1, HID), f32)],
        in_specs=[
            in_vmem, in_vmem, in_vmem, pl.BlockSpec(memory_space=pltpu.SMEM),
            anywhere, in_vmem, anywhere, anywhere,
        ],
        out_specs=[in_vmem] * 3,
        scratch_shapes=[
            vm((ROWS, 128), bf16), vm((REPS, ROWS, 128), bf16), vm((ROWS, REPORTS), bf16),
            vm((512, HID), bf16), vm((HID, 512), bf16), vm((SUB, 512, NLON), bf16),
            vm((4, CH, ROWS), bf16), vm((128, ROWS), f32),
            vm((4, 16, ROWS), f32), vm((4, 8, ROWS), f32), vm((4, 16, ROWS), f32),
            vm((16, NLON, ROWS), bf16), vm((16, SUB, 16, ROWS), bf16), vm((16, 16, ROWS), bf16),
            vm((16, 8, ROWS), f32), vm((SUB * CH + 16, ROWS), bf16),
            vm((LEVELS, SUB * CH + 16, NLON), f32),
            vm((512, CELLS), bf16), vm((512, HID), bf16), vm((HID, 512), bf16), vm((HID, 1), f32),
            vm((HID, CELLS), bf16), vm((HID, CELLS), bf16), vm((LEVELS, SUB * CH, NLON), bf16),
            vm((4, REPS, 128, 256), bf16), vm((4, REPS - 1, 128, 256), bf16),
            vm((ROWS, 128), bf16), vm((ROWS, 128), bf16),
            vm((GROWS, 128), bf16), vm((2048, 128), bf16), vm((512, 128), bf16), vm((64, 128), bf16),
            vm((1, 2048, 128), bf16), vm((3, 512, 128), bf16), vm((7, 64, 128), bf16), vm((3, 16, 128), bf16),
            vm((GROWS, 128), bf16),
            vm((CORES, 8, 128), f32), vm((YS, 8, 128), f32), vm((ZS, 8, 128), f32), vm((REPS, 8, 128), f32),
            dma((3,)), dma, dma, dma, dma, dma((6,)), dma((6,)), dma((12,)), dma((12,)),
            dma((14,)), dma((14,)), dma((14,)), dma((14,)), dma((14,)), dma((14,)),
        ],
        compiler_params=pltpu.CompilerParams(
            collective_id=0, has_side_effects=True, vmem_limit_bytes=60 << 20
        ),
    )(
        embeddings, route.reshape(1, REPORTS), place, scales,
        first_weight, first_bias.reshape(1, HID), second_weight, out_cotangent.transpose(1, 0, 2),
    )
    return (
        gradient, grads[0:512].astype(f32), bias.reshape(HID), grads[512:1024].astype(f32),
    )


def solution(mesh):
    return jax.shard_map(
        on_device,
        mesh=mesh,
        in_specs=(
            P("rep", "band"),
            P("band", None),
            P(None, "band"),
            P(),
            P(),
            P(),
            P(),
            P(None, ("band", "rep"), None),
        ),
        out_specs=(P("rep", "band"), P(), P(), P()),
        check_vma=False,
    )
```

time: 114 us -> 88.7 us (0.78)
  Pallas kernels: 102 us -> 83.8 us
  local copies, waits for them, and re-layouts: 10.2 us -> 1.25 us
  other arithmetic: 0.14 us -> 2.84 us
    pallas_call x3 -> x1, Pallas kernels: 102 us -> 83.8 us  [on_device(): pl.pallas_call(grid_kernel, out_shape=[sds((PART, REPORTS), f32), sds((10...]
    unnamed x21 -> x6, local copies, waits for them, and re-layouts: 6.38 us -> 1.25 us
    convert_element_type x1, other arithmetic: 0.14 us -> 2.84 us  [on_device(): grads[512:1024].astype(f32)]
    slice x3 -> x0, local copies, waits for them, and re-layouts: 1.49 us -> none  [on_device(): return (gradient, both[0], bias_total[0:4].reshape(HID), both[1])]
    squeeze x1 -> x0, local copies, waits for them, and re-layouts: 1.49 us -> none  [on_device(): return (gradient, both[0], bias_total[0:4].reshape(HID), both[1])]
where the time goes in v2:
time: 88.7 us; the launch traced here: 88.5 us
  Pallas kernels  83.8 us (94%)
  other arithmetic  2.84 us (3%)
  local copies, waits for them, and re-layouts  1.25 us (1%)
    pallas_call x1, Pallas kernels, on_device(): pl.pallas_call(grid_kernel, out_shape=[sds((PART, REPORTS), f32), sds((10...  83.8 us
    convert_element_type x1, other arithmetic, on_device(): grads[512:1024].astype(f32)  2.84 us

profile of v2, /device:TPU:1, one launch (start us, length us, event | category | flops | bytes accessed | tf_op | source)
XLA Modules:
  0.0 88.5 jit_solution(5166846435269774263)
XLA Ops:
  0.6 83.8 %shard_map.111 = (f32[32,512]{1,0:T(8,128)}, bf16[1024,512]{1,0:T(8,128)(2,1)}, f32[1,512]{1,0:T(1,128)}) custom-call(bf16[32,512]{1,0:T(8,128)(2,1)} %emb_ref.1, s32[1,512]{1,0:T(1,128)} %bitcast.5, bf16[2,512]{1,0:T(2,128)(2,1)} %place_ref.1, f32[4]{0:T(128)} %scales_ref.1, bf16[512,512]{1,0:T(8,128)(2,1)} %w1_hbm.1, f32[1,512]{1,0:T(1,128)} %bitcast.6, ...), custom_call_target="tpu_custom_call" | custom-call | tf_op jit(solution)/shard_map/pallas_call | solution.py:512
  84.4 0.0 copy-start
  84.4 2.8 %slice_convert_fusion = (f32[512,512]{1,0:T(8,128)}, f32[512,512]{1,0:T(8,128)}) fusion(bf16[1024,512]{1,0:T(8,128)(2,1)} %get-tuple-element.8), kind=kLoop, calls=%fused_computation | loop fusion | flops 524288 | bytes 3145728 | tf_op jit(solution)/shard_map/convert_element_type | solution.py:547
  87.3 0.0 copy-done
  87.3 0.0 copy-start.1
  87.3 0.6 copy.14
  87.9 0.0 copy-done.1
  87.9 0.6 copy.15
Async XLA Ops:
  84.4 2.9 %copy-start = (f32[32,512]{1,0:T(8,128)S(1)}, f32[32,512]{1,0:T(8,128)}, u32[]{:S(2)}) copy-start(f32[32,512]{1,0:T(8,128)} %get-tuple-element.16) | copy-start | bytes 196612
  87.3 0.7 copy-start.1

commit v3 on v2

--- a/solution.py
+++ b/solution.py
@@ -71,23 +71,6 @@
             jnp.where((col == owner) & (mine < lane), 1.0, 0.0), axis=0, keepdims=True
         )
     return owner, rank
-
-
-def greet(me, rep):
-    barrier = pltpu.get_barrier_semaphore()
-
-    def band_peer(d, carry):
-        pl.semaphore_signal(
-            barrier, inc=1, device_id=(lax.rem(me + d, BANDS), rep), device_id_type=MESH
-        )
-        return carry
-
-    lax.fori_loop(1, BANDS, band_peer, 0)
-    for d in range(1, REPS):
-        pl.semaphore_signal(
-            barrier, inc=1, device_id=(me, lax.rem(rep + d, REPS)), device_id_type=MESH
-        )
-    return barrier
 
 
 def send_tiles(me, rep, table, landing, send_sem, recv_sem):
@@ -198,11 +181,12 @@
 
 def grid_kernel(
     emb_ref, route_ref, place_ref, scales_ref, w1_hbm, b1_ref, w2_hbm, cot_hbm,
-    eg_ref, grads_ref, bout_ref,
+    eg_ref, first_ref, second_ref, bout_ref,
     table, rr_ref, pick_ref, w1_ref, w2_ref, cot_ref,
     emb_t, expand, base_ref, east_ref, valid_ref, col_ref, rk_ref, mix_ref, rowf_ref, w_ref, acc_ref,
     feat_ref, w1p_ref, w1t_ref, bcol_ref, hid_ref, pg_ref, sg_ref,
-    d_out, d_in, table2, landing, g0, g1, g2, g3, in_c, in_y, in_z, in_x, full_ref, bc, by, bz, bx,
+    d_out, d_far, d_near, d_sum, d_last, table2, landing, g0, g1, g2, g3, in_c, in_z, in_x,
+    y_far, y_near, y_sum, y_last, full_ref, bc, by, bz, bx, seen_y, seen_c,
     loads, ssem, rsem, ssem2, rsem2, xs, xr, ds, dr, gs, gr, bs, br, as_, ar,
 ):
     me = lax.axis_index("band")
@@ -259,6 +243,57 @@
         for copy in copies:
             copy.wait()
 
+    def ring_reduce(chunk, bufs, sems, base, peer):
+        send, recv = sems
+        far, near = bufs[0], bufs[1]
+        right, left = peer(1), peer(3)
+        return [
+            start(chunk(2, 0), far.at[0], send.at[base], recv.at[base], right),
+            start(chunk(2, 1), far.at[1], send.at[base + 1], recv.at[base + 1], left),
+            start(chunk(1, 1), near.at[0], send.at[base + 2], recv.at[base + 2], right),
+            start(chunk(3, 0), near.at[1], send.at[base + 3], recv.at[base + 3], left),
+        ]
+
+    def ring_relay(copies, chunk, bufs, sems, base, peer):
+        send, recv = sems
+        far, out, last = bufs[0], bufs[2], bufs[3]
+        relayed = []
+        for h, k in ((0, 1), (1, 3)):
+            copies[h].wait()
+            out[h] = (chunk(k, h)[...].astype(f32) + far[h].astype(f32)).astype(bf16)
+            relayed.append(start(out.at[h], last.at[h], send.at[base + 4 + h], recv.at[base + 4 + h], peer(k)))
+        return copies[2:] + relayed
+
+    def ring_total(copies, chunk, bufs):
+        near, last = bufs[1], bufs[3]
+        finish(copies)
+        return [
+            chunk(0, h)[...].astype(f32) + last[h].astype(f32) + near[1 - h].astype(f32) for h in range(2)
+        ]
+
+    def ring_gather(piece, sems, base, peer):
+        send, recv = sems
+        right, left = peer(1), peer(3)
+        one = start(piece(0, 0), piece(0, 0), send.at[base], recv.at[base], right)
+        two = start(piece(0, 1), piece(0, 1), send.at[base + 1], recv.at[base + 1], left)
+        three = start(piece(0, 1), piece(0, 1), send.at[base + 2], recv.at[base + 2], right)
+        four = start(piece(0, 0), piece(0, 0), send.at[base + 3], recv.at[base + 3], left)
+
+        def forward():
+            one.wait_recv()
+            five = start(piece(3, 0), piece(3, 0), send.at[base + 4], recv.at[base + 4], right)
+            two.wait_recv()
+            six = start(piece(1, 1), piece(1, 1), send.at[base + 5], recv.at[base + 5], left)
+
+            def rest():
+                one.wait_send()
+                two.wait_send()
+                finish([three, four, five, six])
+
+            return rest
+
+        return forward
+
     def spread_out(offset, size, n, peer, base):
         at = pl.ds(pl.multiple_of(offset, size), size)
         return [
@@ -266,7 +301,11 @@
             for d in range(1, n)
         ]
 
-    barrier = greet(me, rep)
+    barrier = pltpu.get_barrier_semaphore()
+    lines = ((core_peer, CORES), (y_peer, YS), (z_peer, ZS), (x_peer, REPS))
+    for peer, n in lines:
+        for d in range(1, n):
+            pl.semaphore_signal(barrier, inc=1, device_id=peer(d), device_id_type=MESH)
     held = []
     for k, (src, dst) in enumerate(((w1_hbm, w1_ref), (w2_hbm, w2_ref), (cot_hbm, cot_ref))):
         copy = pltpu.make_async_copy(src, dst, loads.at[k])
@@ -275,7 +314,12 @@
 
     owner, rank = report_ranks(route_ref)
     within = build_table(emb_ref, place_ref, owner, rank, pick_ref, table)
-    pl.semaphore_wait(barrier, BANDS - 1 + REPS - 1)
+    pl.semaphore_wait(barrier, sum(n - 1 for _, n in lines))
+    for d in range(1, YS):
+        pl.semaphore_signal(seen_y, inc=1, device_id=y_peer(d), device_id_type=MESH)
+    pl.semaphore_wait(seen_y, YS - 1)
+    pl.semaphore_signal(seen_c, inc=1, device_id=core_peer(1), device_id_type=MESH)
+    pl.semaphore_wait(seen_c, 1)
     mine = rr_ref.at[rep]
     send_tiles(me, rep, table, mine, ssem, rsem)
     own = rows_at(me, TILE)
@@ -290,19 +334,11 @@
 
     done = tiles_done(me, rep, table, mine, ssem, rsem)
     done.wait_recv()
-    x_copies = []
-    for half in range(2):
-        rows = pl.ds(half * 512, 512)
-        x_copies.append(
-            [
-                start(
-                    rr_ref.at[rep, rows], rr_ref.at[rep, rows],
-                    xs.at[half * 3 + d - 1], xr.at[half * 3 + d - 1], x_peer(d),
-                )
-                for d in range(1, REPS)
-            ]
-        )
-
+    def report_piece(half):
+        return lambda k, h: rr_ref.at[lax.rem(rep + k, REPS), pl.ds(half * 512 + h * 256, 256)]
+
+    first_half = ring_gather(report_piece(0), (xs, xr), 0, x_peer)()
+    forward_second = ring_gather(report_piece(1), (xs, xr), 6, x_peer)
     ident = eye(128)
     group = one_where(
         ((iota((128, 128), 0) >> 4) == (iota((128, 128), 1) >> 4)) & ((iota((128, 128), 0) & 15) == 15)
@@ -317,11 +353,13 @@
         kernels(it, scales_ref, base_ref, east_ref, valid_ref, col_ref, rk_ref, mix_ref, rowf_ref)
         return carry
 
-    lax.fori_loop(0, 16, make, 0)
+    lax.fori_loop(0, 8, make, 0)
+    second_half = forward_second()
+    lax.fori_loop(8, 16, make, 0)
 
     for half in range(2):
         lanes = slice(half * 512, (half + 1) * 512)
-        finish(x_copies[half])
+        (first_half, second_half)[half]()
         for q in range(REPS):
             turned = dot_nt(ident, rr_ref[q, lanes, :]).astype(bf16)
             for s in range(4):
@@ -407,19 +445,20 @@
             return carry
 
         lax.fori_loop(0, 4, one_group, 0)
-        return [
-            start(
-                d_out.at[n, lax.rem(rep + d, REPS)], d_in.at[n, d - 1],
-                ds.at[n * 3 + d - 1], dr.at[n * 3 + d - 1], x_peer(d),
-            )
-            for d in range(1, REPS)
-        ]
+        return ring_reduce(slot_part(n), slot_bufs(n), (ds, dr), n * 6, x_peer)
+
+    def slot_part(n):
+        return lambda k, h: d_out.at[n, lax.rem(rep + k, REPS), pl.ds(h * 64, 64)]
+
+    def slot_bufs(n):
+        return d_far.at[n], d_near.at[n], d_sum.at[n], d_last.at[n]
+
+    def relay(n, copies):
+        return ring_relay(copies, slot_part(n), slot_bufs(n), (ds, dr), n * 6, x_peer)
 
     def to_feeds(n, copies):
-        finish(copies)
-        total = d_out[n, rep].astype(f32)
-        for d in range(REPS - 1):
-            total = total + d_in[n, d].astype(f32)
+        halves = ring_total(copies, slot_part(n), slot_bufs(n))
+        total = jnp.concatenate(halves, axis=0)
         table2[n * 256 : (n + 1) * 256, :] = jnp.transpose(total).astype(bf16)
 
         def send(j, carry):
@@ -440,31 +479,39 @@
 
         lax.fori_loop(0, 16, send, 0)
 
-    d0 = spread(0)
+    def y_part(k, h):
+        return g1.at[pl.ds(pl.multiple_of(lax.rem(y + k, YS) * 512 + h * 256, 256), 256)]
+
+    y_bufs = (y_far, y_near, y_sum, y_last)
+
     finish(c_copies)
     g1[...] = (g0[rows_at(core, 2048), :].astype(f32) + in_c[0].astype(f32)).astype(bf16)
-    y_copies = scatter(g1, in_y, 512, YS, y, y_peer, 1)
+    y_copies = ring_reduce(y_part, y_bufs, (gs, gr), 1, y_peer)
     finish(c_bias)
     y_bias = bias_round(bias_sum(bc, CORES), by, YS, y, y_peer, 1)
+    d0 = spread(0)
+    y_copies = ring_relay(y_copies, y_part, y_bufs, (gs, gr), 1, y_peer)
     d1 = spread(1)
-    d2 = spread(2)
-    to_feeds(0, d0)
-    finish(y_copies)
-    total = g1[rows_at(y, 512), :].astype(f32)
-    for d in range(YS - 1):
-        total = total + in_y[d].astype(f32)
-    g2[...] = total.astype(bf16)
-    z_copies = scatter(g2, in_z, 64, ZS, z, z_peer, 4)
+    d0 = relay(0, d0)
+    y_sums = ring_total(y_copies, y_part, y_bufs)
+    for h in range(2):
+        g2[h * 256 : (h + 1) * 256, :] = y_sums[h].astype(bf16)
+    z_copies = scatter(g2, in_z, 64, ZS, z, z_peer, 7)
     finish(y_bias)
     z_bias = bias_round(bias_sum(by, YS), bz, ZS, z, z_peer, 4)
+    d2 = spread(2)
+    d1 = relay(1, d1)
+    to_feeds(0, d0)
     d3 = spread(3)
+    d2 = relay(2, d2)
     to_feeds(1, d1)
     finish(z_copies)
     total = g2[rows_at(z, 64), :].astype(f32)
     for d in range(ZS - 1):
         total = total + in_z[d].astype(f32)
     g3[...] = total.astype(bf16)
-    x_copies = scatter(g3, in_x, 16, REPS, rep, x_peer, 11)
+    x_copies = scatter(g3, in_x, 16, REPS, rep, x_peer, 14)
+    d3 = relay(3, d3)
     finish(z_bias)
     x_bias = bias_round(bias_sum(bz, ZS), bx, REPS, rep, x_peer, 11)
     to_feeds(2, d2)
@@ -484,7 +531,12 @@
     to_feeds(3, d3)
     landing[own, :] = table2[own, :]
     finish(copies)
-    copies = spread_out(core * 2048 + y * 512, 512, YS, y_peer, 10)
+
+    def y_block(k, h):
+        at = core * 2048 + lax.rem(y + k, YS) * 512 + h * 256
+        return full_ref.at[pl.ds(pl.multiple_of(at, 256), 256)]
+
+    y_gathered = ring_gather(y_block, (as_, ar), 10, y_peer)()
     tiles_done(me, rep, table2, landing, ssem2, rsem2).wait()
     turned = dot_nt(ident, landing[...]).astype(bf16)
     found = dot(turned, pick_ref[...])
@@ -492,10 +544,12 @@
     for s in range(4):
         gradient = gradient + jnp.where(within == float(s), found[s * PART : (s + 1) * PART, :], 0.0)
     eg_ref[...] = gradient
-    finish(copies)
-    finish(spread_out(core * 2048, 2048, CORES, core_peer, 13))
+    y_gathered()
+    finish(spread_out(core * 2048, 2048, CORES, core_peer, 16))
     for c in range(4):
-        grads_ref[:, c * 128 : (c + 1) * 128] = full_ref[c * 1024 : (c + 1) * 1024, :]
+        lanes = slice(c * 128, (c + 1) * 128)
+        first_ref[:, lanes] = full_ref[c * 1024 : c * 1024 + 512, :].astype(f32)
+        second_ref[:, lanes] = full_ref[c * 1024 + 512 : (c + 1) * 1024, :].astype(f32)
 
 
 def sds(shape, dtype):
@@ -509,14 +563,14 @@
     vm = pltpu.VMEM
     in_vmem = pl.BlockSpec(memory_space=pltpu.VMEM)
     anywhere = pl.BlockSpec(memory_space=pl.ANY)
-    gradient, grads, bias = pl.pallas_call(
+    gradient, first, second, bias = pl.pallas_call(
         grid_kernel,
-        out_shape=[sds((PART, REPORTS), f32), sds((1024, 512), bf16), sds((1, HID), f32)],
+        out_shape=[sds((PART, REPORTS), f32), sds((512, 512), f32), sds((512, 512), f32), sds((1, HID), f32)],
         in_specs=[
             in_vmem, in_vmem, in_vmem, pl.BlockSpec(memory_space=pltpu.SMEM),
             anywhere, in_vmem, anywhere, anywhere,
         ],
-        out_specs=[in_vmem] * 3,
+        out_specs=[in_vmem] * 4,
         scratch_shapes=[
             vm((ROWS, 128), bf16), vm((REPS, ROWS, 128), bf16), vm((ROWS, REPORTS), bf16),
             vm((512, HID), bf16), vm((HID, 512), bf16), vm((SUB, 512, NLON), bf16),
@@ -527,14 +581,16 @@
             vm((LEVELS, SUB * CH + 16, NLON), f32),
             vm((512, CELLS), bf16), vm((512, HID), bf16), vm((HID, 512), bf16), vm((HID, 1), f32),
             vm((HID, CELLS), bf16), vm((HID, CELLS), bf16), vm((LEVELS, SUB * CH, NLON), bf16),
-            vm((4, REPS, 128, 256), bf16), vm((4, REPS - 1, 128, 256), bf16),
+            vm((4, REPS, 128, 256), bf16), *([vm((4, 2, 64, 256), bf16)] * 4),
             vm((ROWS, 128), bf16), vm((ROWS, 128), bf16),
             vm((GROWS, 128), bf16), vm((2048, 128), bf16), vm((512, 128), bf16), vm((64, 128), bf16),
-            vm((1, 2048, 128), bf16), vm((3, 512, 128), bf16), vm((7, 64, 128), bf16), vm((3, 16, 128), bf16),
+            vm((1, 2048, 128), bf16), vm((7, 64, 128), bf16), vm((3, 16, 128), bf16),
+            *([vm((2, 256, 128), bf16)] * 4),
             vm((GROWS, 128), bf16),
             vm((CORES, 8, 128), f32), vm((YS, 8, 128), f32), vm((ZS, 8, 128), f32), vm((REPS, 8, 128), f32),
-            dma((3,)), dma, dma, dma, dma, dma((6,)), dma((6,)), dma((12,)), dma((12,)),
-            dma((14,)), dma((14,)), dma((14,)), dma((14,)), dma((14,)), dma((14,)),
+            pltpu.SemaphoreType.REGULAR, pltpu.SemaphoreType.REGULAR,
+            dma((3,)), dma, dma, dma, dma, dma((12,)), dma((12,)), dma((24,)), dma((24,)),
+            dma((17,)), dma((17,)), dma((14,)), dma((14,)), dma((17,)), dma((17,)),
         ],
         compiler_params=pltpu.CompilerParams(
             collective_id=0, has_side_effects=True, vmem_limit_bytes=60 << 20
@@ -543,9 +599,7 @@
         embeddings, route.reshape(1, REPORTS), place, scales,
         first_weight, first_bias.reshape(1, HID), second_weight, out_cotangent.transpose(1, 0, 2),
     )
-    return (
-        gradient, grads[0:512].astype(f32), bias.reshape(HID), grads[512:1024].astype(f32),
-    )
+    return (gradient, first, bias.reshape(HID), second)
 
 
 def solution(mesh):

time: 88.7 us -> 97 us (1.094)
  Pallas kernels: 83.8 us -> 90.7 us
  local copies, waits for them, and re-layouts: 1.25 us -> 5.38 us
  other arithmetic: 2.84 us -> 0 us
    pallas_call x1, Pallas kernels: 83.8 us -> 90.7 us  [on_device(): pl.pallas_call(grid_kernel, out_shape=[sds((PART, REPORTS), f32), sds((51...]
    unnamed x6 -> x8, local copies, waits for them, and re-layouts: 1.25 us -> 5.38 us
    convert_element_type x1 -> x0, other arithmetic: 2.84 us -> none  [on_device(): grads[512:1024].astype(f32)]
where the time goes in v3:
time: 97 us; the launch traced here: 96.8 us
  Pallas kernels  90.7 us (94%)
  local copies, waits for them, and re-layouts  5.38 us (6%)
    pallas_call x1, Pallas kernels, on_device(): pl.pallas_call(grid_kernel, out_shape=[sds((PART, REPORTS), f32), sds((51...  90.7 us
    unnamed x8, local copies, waits for them, and re-layouts  5.38 us

profile of v3, /device:TPU:1, one launch (start us, length us, event | category | flops | bytes accessed | tf_op | source)
XLA Modules:
  0.0 96.8 jit_solution(4845017787909440436)
XLA Ops:
  0.6 90.7 %shard_map.111 = (f32[32,512]{1,0:T(8,128)}, f32[512,512]{1,0:T(8,128)}, f32[512,512]{1,0:T(8,128)}, f32[1,512]{1,0:T(1,128)}) custom-call(bf16[32,512]{1,0:T(8,128)(2,1)} %emb_ref.1, s32[1,512]{1,0:T(1,128)} %bitcast.5, bf16[2,512]{1,0:T(2,128)(2,1)} %place_ref.1, f32[4]{0:T(128)} %scales_ref.1, bf16[512,512]{1,0:T(8,128)(2,1)} %w1_hbm.1, ...), custom_call_target="tpu_custom_call" | custom-call | tf_op jit(solution)/shard_map/pallas_call | solution.py:566
  91.4 1.5 %copy.16 = f32[32,512]{1,0:T(8,128)} copy(f32[32,512]{1,0:T(8,128)} %get-tuple-element.16) | data formatting | bytes 131072
  92.9 0.0 copy-start.1
  92.9 0.0 copy-start
  92.9 2.4 %copy.17 = f32[512,512]{1,0:T(8,128)} copy(f32[512,512]{1,0:T(8,128)} %get-tuple-element.17) | data formatting | bytes 2097152
  95.2 0.0 copy-done.1
  95.2 0.6 copy.18
  95.8 0.0 copy-done
  95.8 1.0 %copy.19 = f32[512,512]{1,0:T(8,128)} copy(f32[512,512]{1,0:T(8,128)S(1)} %copy-done) | data formatting | bytes 2097152
Async XLA Ops:
  92.9 2.4 %copy-start.1 = (f32[1,512]{1,0:T(1,128)S(1)}, f32[1,512]{1,0:T(1,128)}, u32[]{:S(2)}) copy-start(f32[1,512]{1,0:T(1,128)} %get-tuple-element.10) | copy-start | bytes 6148
  92.9 2.9 %copy-start = (f32[512,512]{1,0:T(8,128)S(1)}, f32[512,512]{1,0:T(8,128)}, u32[]{:S(2)}) copy-start(f32[512,512]{1,0:T(8,128)} %get-tuple-element.19) | copy-start | bytes 3145732

commit v4 on v2

--- a/solution.py
+++ b/solution.py
@@ -202,8 +202,8 @@
     table, rr_ref, pick_ref, w1_ref, w2_ref, cot_ref,
     emb_t, expand, base_ref, east_ref, valid_ref, col_ref, rk_ref, mix_ref, rowf_ref, w_ref, acc_ref,
     feat_ref, w1p_ref, w1t_ref, bcol_ref, hid_ref, pg_ref, sg_ref,
-    d_out, d_in, table2, landing, g0, g1, g2, g3, in_c, in_y, in_z, in_x, full_ref, bc, by, bz, bx,
-    loads, ssem, rsem, ssem2, rsem2, xs, xr, ds, dr, gs, gr, bs, br, as_, ar,
+    d_out, d_in, table2, landing, g0, g1, g2, in_c, in_y, in_g, full_ref, bc, by, bz, bx,
+    loads, ssem, rsem, ssem2, rsem2, vs, vr, vs2, vr2, xs, xr, ds, dr, gs, gr, bs, br, as_, ar,
 ):
     me = lax.axis_index("band")
     rep = lax.axis_index("rep")
@@ -233,15 +233,6 @@
     def rows_at(index, size):
         return pl.ds(pl.multiple_of(index * size, size), size)
 
-    def scatter(src, dst, size, n, mine, peer, base):
-        return [
-            start(
-                src.at[rows_at(lax.rem(mine + d, n), size)], dst.at[d - 1],
-                gs.at[base + d - 1], gr.at[base + d - 1], peer(d),
-            )
-            for d in range(1, n)
-        ]
-
     def bias_round(value, slots, n, mine, peer, base):
         slots[mine] = value
         return [
@@ -259,12 +250,50 @@
         for copy in copies:
             copy.wait()
 
-    def spread_out(offset, size, n, peer, base):
-        at = pl.ds(pl.multiple_of(offset, size), size)
-        return [
-            start(full_ref.at[at], full_ref.at[at], as_.at[base + d - 1], ar.at[base + d - 1], peer(d))
-            for d in range(1, n)
-        ]
+    def ring_gather(piece, sems, base, peer):
+        send, recv = sems
+        right, left = peer(1), peer(3)
+        one = start(piece(0, 0), piece(0, 0), send.at[base], recv.at[base], right)
+        two = start(piece(0, 1), piece(0, 1), send.at[base + 1], recv.at[base + 1], left)
+        three = start(piece(0, 1), piece(0, 1), send.at[base + 2], recv.at[base + 2], right)
+        four = start(piece(0, 0), piece(0, 0), send.at[base + 3], recv.at[base + 3], left)
+
+        def forward():
+            one.wait_recv()
+            five = start(piece(3, 0), piece(3, 0), send.at[base + 4], recv.at[base + 4], right)
+            two.wait_recv()
+            six = start(piece(1, 1), piece(1, 1), send.at[base + 5], recv.at[base + 5], left)
+
+            def rest():
+                one.wait_send()
+                two.wait_send()
+                finish([three, four, five, six])
+
+            return rest
+
+        return forward
+
+    group_at = z * REPS + rep
+
+    def group_peer(j):
+        return y * (CORES * ZS) + (j >> 2) * CORES + core, j & 3
+
+    def to_group(src, src_at, dst, dst_at, send, recv):
+        def one(d, carry):
+            j = lax.rem(group_at + d, ZS * REPS)
+            pltpu.make_async_remote_copy(
+                src_ref=src.at[pl.ds(pl.multiple_of(src_at(j), TILE), TILE)],
+                dst_ref=dst.at[pl.ds(pl.multiple_of(dst_at, TILE), TILE)],
+                send_sem=send, recv_sem=recv, device_id=group_peer(j), device_id_type=MESH,
+            ).start()
+            return carry
+
+        lax.fori_loop(1, ZS * REPS, one, 0)
+        rows = pl.ds(0, (ZS * REPS - 1) * TILE)
+        return pltpu.make_async_remote_copy(
+            src_ref=src.at[rows], dst_ref=dst.at[rows], send_sem=send, recv_sem=recv,
+            device_id=group_peer(lax.rem(group_at + 1, ZS * REPS)), device_id_type=MESH,
+        )
 
     barrier = greet(me, rep)
     held = []
@@ -290,19 +319,11 @@
 
     done = tiles_done(me, rep, table, mine, ssem, rsem)
     done.wait_recv()
-    x_copies = []
-    for half in range(2):
-        rows = pl.ds(half * 512, 512)
-        x_copies.append(
-            [
-                start(
-                    rr_ref.at[rep, rows], rr_ref.at[rep, rows],
-                    xs.at[half * 3 + d - 1], xr.at[half * 3 + d - 1], x_peer(d),
-                )
-                for d in range(1, REPS)
-            ]
-        )
-
+    def report_piece(half):
+        return lambda k, h: rr_ref.at[lax.rem(rep + k, REPS), pl.ds(half * 512 + h * 256, 256)]
+
+    first_half = ring_gather(report_piece(0), (xs, xr), 0, x_peer)()
+    forward_second = ring_gather(report_piece(1), (xs, xr), 6, x_peer)
     ident = eye(128)
     group = one_where(
         ((iota((128, 128), 0) >> 4) == (iota((128, 128), 1) >> 4)) & ((iota((128, 128), 0) & 15) == 15)
@@ -317,11 +338,13 @@
         kernels(it, scales_ref, base_ref, east_ref, valid_ref, col_ref, rk_ref, mix_ref, rowf_ref)
         return carry
 
-    lax.fori_loop(0, 16, make, 0)
+    lax.fori_loop(0, 8, make, 0)
+    second_half = forward_second()
+    lax.fori_loop(8, 16, make, 0)
 
     for half in range(2):
         lanes = slice(half * 512, (half + 1) * 512)
-        finish(x_copies[half])
+        (first_half, second_half)[half]()
         for q in range(REPS):
             turned = dot_nt(ident, rr_ref[q, lanes, :]).astype(bf16)
             for s in range(4):
@@ -381,7 +404,12 @@
     bias_tile = jnp.concatenate(
         [bias[0:1, c * 128 : (c + 1) * 128] for c in range(4)] + [jnp.zeros((4, 128), f32)], axis=0
     )
-    c_copies = scatter(g0, in_c, 2048, CORES, core, core_peer, 0)
+    c_copies = []
+    for d in (1, 2, 3, 0):
+        k = lax.rem(y + d, YS)
+        c_copies.append(
+            start(g0.at[rows_at((1 - core) * YS + k, 512)], in_c.at[rows_at(k, 512)], gs.at[d], gr.at[d], core_peer(1))
+        )
     c_bias = bias_round(bias_tile, bc, CORES, core, core_peer, 0)
 
     for i in range(SUB):
@@ -441,50 +469,64 @@
         lax.fori_loop(0, 16, send, 0)
 
     d0 = spread(0)
-    finish(c_copies)
-    g1[...] = (g0[rows_at(core, 2048), :].astype(f32) + in_c[0].astype(f32)).astype(bf16)
-    y_copies = scatter(g1, in_y, 512, YS, y, y_peer, 1)
+    y_copies = []
+    for d, copy in zip((1, 2, 3, 0), c_copies):
+        k = lax.rem(y + d, YS)
+        copy.wait()
+        g1[rows_at(k, 512), :] = (
+            g0[rows_at(core * YS + k, 512), :].astype(f32) + in_c[rows_at(k, 512), :].astype(f32)
+        ).astype(bf16)
+        if d:
+            y_copies.append(start(g1.at[rows_at(k, 512)], in_y.at[d - 1], gs.at[3 + d], gr.at[3 + d], y_peer(d)))
     finish(c_bias)
     y_bias = bias_round(bias_sum(bc, CORES), by, YS, y, y_peer, 1)
     d1 = spread(1)
     d2 = spread(2)
-    to_feeds(0, d0)
     finish(y_copies)
     total = g1[rows_at(y, 512), :].astype(f32)
     for d in range(YS - 1):
         total = total + in_y[d].astype(f32)
     g2[...] = total.astype(bf16)
-    z_copies = scatter(g2, in_z, 64, ZS, z, z_peer, 4)
+    own_tile = rows_at(group_at, TILE)
+    in_g[own_tile, :] = g2[own_tile, :]
+    scattered = to_group(g2, lambda j: j * TILE, in_g, group_at * TILE, vs, vr)
     finish(y_bias)
     z_bias = bias_round(bias_sum(by, YS), bz, ZS, z, z_peer, 4)
+    to_feeds(0, d0)
     d3 = spread(3)
+    scattered.wait()
+    total = in_g[0:TILE, :].astype(f32)
+    for j in range(1, ZS * REPS):
+        total = total + in_g[j * TILE : (j + 1) * TILE, :].astype(f32)
+    block_at = core * 2048 + y * 512
+    full_ref[pl.ds(pl.multiple_of(block_at + group_at * TILE, TILE), TILE), :] = total.astype(bf16)
+    gathered = to_group(
+        full_ref, lambda j: block_at + group_at * TILE, full_ref, block_at + group_at * TILE, vs2, vr2
+    )
     to_feeds(1, d1)
-    finish(z_copies)
-    total = g2[rows_at(z, 64), :].astype(f32)
-    for d in range(ZS - 1):
-        total = total + in_z[d].astype(f32)
-    g3[...] = total.astype(bf16)
-    x_copies = scatter(g3, in_x, 16, REPS, rep, x_peer, 11)
     finish(z_bias)
     x_bias = bias_round(bias_sum(bz, ZS), bx, REPS, rep, x_peer, 11)
     to_feeds(2, d2)
-    finish(x_copies)
-    total = g3[rows_at(rep, 16), :].astype(f32)
-    for d in range(REPS - 1):
-        total = total + in_x[d].astype(f32)
-    at_z = core * 2048 + y * 512 + z * 64
-    full_ref[pl.ds(pl.multiple_of(at_z + rep * 16, 16), 16), :] = total.astype(bf16)
-    copies = spread_out(at_z + rep * 16, 16, REPS, x_peer, 0)
+    gathered.wait()
+
+    def block(k):
+        return full_ref.at[rows_at(core * YS + k, 512)]
+
+    def to_core(d):
+        k = lax.rem(y + YS - d, YS)
+        return start(block(k), block(k), as_.at[3 + d], ar.at[3 + d], core_peer(1))
+
+    blocks = [start(block(y), block(y), as_.at[d - 1], ar.at[d - 1], y_peer(d)) for d in range(1, YS)]
+    crossing = [to_core(0)]
+    to_feeds(3, d3)
+    landing[own, :] = table2[own, :]
     finish(x_bias)
     bias_total = bias_sum(bx, REPS)
     for c in range(4):
         bout_ref[:, c * 128 : (c + 1) * 128] = bias_total[c : c + 1, :]
-    finish(copies)
-    copies = spread_out(at_z, 64, ZS, z_peer, 3)
-    to_feeds(3, d3)
-    landing[own, :] = table2[own, :]
-    finish(copies)
-    copies = spread_out(core * 2048 + y * 512, 512, YS, y_peer, 10)
+    for d in (1, 3, 2):
+        blocks[d - 1].wait()
+        crossing.append(to_core(d))
     tiles_done(me, rep, table2, landing, ssem2, rsem2).wait()
     turned = dot_nt(ident, landing[...]).astype(bf16)
     found = dot(turned, pick_ref[...])
@@ -492,8 +534,7 @@
     for s in range(4):
         gradient = gradient + jnp.where(within == float(s), found[s * PART : (s + 1) * PART, :], 0.0)
     eg_ref[...] = gradient
-    finish(copies)
-    finish(spread_out(core * 2048, 2048, CORES, core_peer, 13))
+    finish(crossing)
     for c in range(4):
         grads_ref[:, c * 128 : (c + 1) * 128] = full_ref[c * 1024 : (c + 1) * 1024, :]
 
@@ -529,12 +570,13 @@
             vm((HID, CELLS), bf16), vm((HID, CELLS), bf16), vm((LEVELS, SUB * CH, NLON), bf16),
             vm((4, REPS, 128, 256), bf16), vm((4, REPS - 1, 128, 256), bf16),
             vm((ROWS, 128), bf16), vm((ROWS, 128), bf16),
-            vm((GROWS, 128), bf16), vm((2048, 128), bf16), vm((512, 128), bf16), vm((64, 128), bf16),
-            vm((1, 2048, 128), bf16), vm((3, 512, 128), bf16), vm((7, 64, 128), bf16), vm((3, 16, 128), bf16),
+            vm((GROWS, 128), bf16), vm((2048, 128), bf16), vm((512, 128), bf16),
+            vm((2048, 128), bf16), vm((3, 512, 128), bf16), vm((512, 128), bf16),
             vm((GROWS, 128), bf16),
             vm((CORES, 8, 128), f32), vm((YS, 8, 128), f32), vm((ZS, 8, 128), f32), vm((REPS, 8, 128), f32),
-            dma((3,)), dma, dma, dma, dma, dma((6,)), dma((6,)), dma((12,)), dma((12,)),
-            dma((14,)), dma((14,)), dma((14,)), dma((14,)), dma((14,)), dma((14,)),
+            dma((3,)), dma, dma, dma, dma, dma, dma, dma, dma,
+            dma((12,)), dma((12,)), dma((12,)), dma((12,)),
+            dma((7,)), dma((7,)), dma((14,)), dma((14,)), dma((7,)), dma((7,)),
         ],
         compiler_params=pltpu.CompilerParams(
             collective_id=0, has_side_effects=True, vmem_limit_bytes=60 << 20

time: 88.7 us -> 87.1 us (0.982)
  Pallas kernels: 83.8 us -> 82.2 us
    pallas_call x1, Pallas kernels: 83.8 us -> 82.2 us  [on_device(): pl.pallas_call(grid_kernel, out_shape=[sds((PART, REPORTS), f32), sds((10...]
where the time goes in v4:
time: 87.1 us; the launch traced here: 86.9 us
  Pallas kernels  82.2 us (94%)
  other arithmetic  2.84 us (3%)
  local copies, waits for them, and re-layouts  1.25 us (1%)
    pallas_call x1, Pallas kernels, on_device(): pl.pallas_call(grid_kernel, out_shape=[sds((PART, REPORTS), f32), sds((10...  82.2 us
    convert_element_type x1, other arithmetic, on_device(): grads[512:1024].astype(f32)  2.84 us

profile of v4, /device:TPU:1, one launch (start us, length us, event | category | flops | bytes accessed | tf_op | source)
XLA Modules:
  0.0 86.9 jit_solution(16297266238795898389)
XLA Ops:
  0.6 82.2 %shard_map.111 = (f32[32,512]{1,0:T(8,128)}, bf16[1024,512]{1,0:T(8,128)(2,1)}, f32[1,512]{1,0:T(1,128)}) custom-call(bf16[32,512]{1,0:T(8,128)(2,1)} %emb_ref.1, s32[1,512]{1,0:T(1,128)} %bitcast.5, bf16[2,512]{1,0:T(2,128)(2,1)} %place_ref.1, f32[4]{0:T(128)} %scales_ref.1, bf16[512,512]{1,0:T(8,128)(2,1)} %w1_hbm.1, f32[1,512]{1,0:T(1,128)} %bitcast.6, ...), custom_call_target="tpu_custom_call" | custom-call | tf_op jit(solution)/shard_map/pallas_call | solution.py:553
  82.8 0.0 copy-start
  82.8 2.8 %slice_convert_fusion = (f32[512,512]{1,0:T(8,128)}, f32[512,512]{1,0:T(8,128)}) fusion(bf16[1024,512]{1,0:T(8,128)(2,1)} %get-tuple-element.8), kind=kLoop, calls=%fused_computation | loop fusion | flops 524288 | bytes 3145728 | tf_op jit(solution)/shard_map/convert_element_type | solution.py:589
  85.7 0.0 copy-done
  85.7 0.0 copy-start.1
  85.7 0.6 copy.14
  86.3 0.0 copy-done.1
  86.3 0.6 copy.15
Async XLA Ops:
  82.8 2.9 %copy-start = (f32[32,512]{1,0:T(8,128)S(1)}, f32[32,512]{1,0:T(8,128)}, u32[]{:S(2)}) copy-start(f32[32,512]{1,0:T(8,128)} %get-tuple-element.16) | copy-start | bytes 196612
  85.7 0.7 copy-start.1

commit v5 on v4

--- a/solution.py
+++ b/solution.py
@@ -198,7 +198,7 @@
 
 def grid_kernel(
     emb_ref, route_ref, place_ref, scales_ref, w1_hbm, b1_ref, w2_hbm, cot_hbm,
-    eg_ref, grads_ref, bout_ref,
+    eg_ref, first_ref, second_ref,
     table, rr_ref, pick_ref, w1_ref, w2_ref, cot_ref,
     emb_t, expand, base_ref, east_ref, valid_ref, col_ref, rk_ref, mix_ref, rowf_ref, w_ref, acc_ref,
     feat_ref, w1p_ref, w1t_ref, bcol_ref, hid_ref, pg_ref, sg_ref,
@@ -322,8 +322,7 @@
     def report_piece(half):
         return lambda k, h: rr_ref.at[lax.rem(rep + k, REPS), pl.ds(half * 512 + h * 256, 256)]
 
-    first_half = ring_gather(report_piece(0), (xs, xr), 0, x_peer)()
-    forward_second = ring_gather(report_piece(1), (xs, xr), 6, x_peer)
+    forward_first = ring_gather(report_piece(0), (xs, xr), 0, x_peer)
     ident = eye(128)
     group = one_where(
         ((iota((128, 128), 0) >> 4) == (iota((128, 128), 1) >> 4)) & ((iota((128, 128), 0) & 15) == 15)
@@ -338,13 +337,17 @@
         kernels(it, scales_ref, base_ref, east_ref, valid_ref, col_ref, rk_ref, mix_ref, rowf_ref)
         return carry
 
-    lax.fori_loop(0, 8, make, 0)
-    second_half = forward_second()
-    lax.fori_loop(8, 16, make, 0)
+    lax.fori_loop(0, 16, make, 0)
+    first_half = forward_first()
+    forward_second = ring_gather(report_piece(1), (xs, xr), 6, x_peer)
 
     for half in range(2):
         lanes = slice(half * 512, (half + 1) * 512)
-        (first_half, second_half)[half]()
+        if half == 0:
+            first_half()
+            second_half = forward_second()
+        else:
+            second_half()
         for q in range(REPS):
             turned = dot_nt(ident, rr_ref[q, lanes, :]).astype(bf16)
             for s in range(4):
@@ -468,7 +471,6 @@
 
         lax.fori_loop(0, 16, send, 0)
 
-    d0 = spread(0)
     y_copies = []
     for d, copy in zip((1, 2, 3, 0), c_copies):
         k = lax.rem(y + d, YS)
@@ -480,6 +482,7 @@
             y_copies.append(start(g1.at[rows_at(k, 512)], in_y.at[d - 1], gs.at[3 + d], gr.at[3 + d], y_peer(d)))
     finish(c_bias)
     y_bias = bias_round(bias_sum(bc, CORES), by, YS, y, y_peer, 1)
+    d0 = spread(0)
     d1 = spread(1)
     d2 = spread(2)
     finish(y_copies)
@@ -522,8 +525,8 @@
     landing[own, :] = table2[own, :]
     finish(x_bias)
     bias_total = bias_sum(bx, REPS)
-    for c in range(4):
-        bout_ref[:, c * 128 : (c + 1) * 128] = bias_total[c : c + 1, :]
+    bias_row = jnp.concatenate([bias_total[c : c + 1, :] for c in range(4)], axis=1)
+    eg_ref[PART : PART + 8, :] = jnp.broadcast_to(bias_row, (8, HID))
     for d in (1, 3, 2):
         blocks[d - 1].wait()
         crossing.append(to_core(d))
@@ -533,10 +536,12 @@
     gradient = jnp.zeros((PART, REPORTS), f32)
     for s in range(4):
         gradient = gradient + jnp.where(within == float(s), found[s * PART : (s + 1) * PART, :], 0.0)
-    eg_ref[...] = gradient
+    eg_ref[0:PART, :] = gradient
     finish(crossing)
     for c in range(4):
-        grads_ref[:, c * 128 : (c + 1) * 128] = full_ref[c * 1024 : (c + 1) * 1024, :]
+        lanes = slice(c * 128, (c + 1) * 128)
+        first_ref[:, lanes] = full_ref[c * 1024 : c * 1024 + 512, :]
+        second_ref[:, lanes] = full_ref[c * 1024 + 512 : (c + 1) * 1024, :]
 
 
 def sds(shape, dtype):
@@ -550,9 +555,9 @@
     vm = pltpu.VMEM
     in_vmem = pl.BlockSpec(memory_space=pltpu.VMEM)
     anywhere = pl.BlockSpec(memory_space=pl.ANY)
-    gradient, grads, bias = pl.pallas_call(
+    gradient, first, second = pl.pallas_call(
         grid_kernel,
-        out_shape=[sds((PART, REPORTS), f32), sds((1024, 512), bf16), sds((1, HID), f32)],
+        out_shape=[sds((PART + 8, REPORTS), f32), sds((512, 512), bf16), sds((512, 512), bf16)],
         in_specs=[
             in_vmem, in_vmem, in_vmem, pl.BlockSpec(memory_space=pltpu.SMEM),
             anywhere, in_vmem, anywhere, anywhere,
@@ -585,9 +590,7 @@
         embeddings, route.reshape(1, REPORTS), place, scales,
         first_weight, first_bias.reshape(1, HID), second_weight, out_cotangent.transpose(1, 0, 2),
     )
-    return (
-        gradient, grads[0:512].astype(f32), bias.reshape(HID), grads[512:1024].astype(f32),
-    )
+    return (gradient[0:PART], first.astype(f32), gradient[PART], second.astype(f32))
 
 
 def solution(mesh):

time: 87.1 us -> 88.8 us (1.020)
  local copies, waits for them, and re-layouts: 1.25 us -> 2.77 us
    slice x0 -> x2, local copies, waits for them, and re-layouts: none -> 2.77 us  [the longest x1 1.47 us: on_device(): gradient[0:PART]]
    unnamed x6 -> x2, local copies, waits for them, and re-layouts: 1.25 us -> 0.01 us
    convert_element_type x1 -> x2, other arithmetic: 2.84 us -> 3.3 us  [the longest x1 2.2 us: on_device(): first.astype(f32)]
where the time goes in v5:
time: 88.8 us; the launch traced here: 88.5 us
  Pallas kernels  81.8 us (92%)
  other arithmetic  3.3 us (4%)
  local copies, waits for them, and re-layouts  2.77 us (3%)
    pallas_call x1, Pallas kernels, on_device(): pl.pallas_call(grid_kernel, out_shape=[sds((PART + 8, REPORTS), f32), sds...  81.8 us
    convert_element_type x1, other arithmetic, on_device(): first.astype(f32)  2.2 us

profile of v5, /device:TPU:1, one launch (start us, length us, event | category | flops | bytes accessed | tf_op | source)
XLA Modules:
  0.0 88.5 jit_solution(12398870947998965270)
XLA Ops:
  0.6 81.8 %shard_map.111 = (f32[40,512]{1,0:T(8,128)}, bf16[512,512]{1,0:T(8,128)(2,1)}, bf16[512,512]{1,0:T(8,128)(2,1)}) custom-call(bf16[32,512]{1,0:T(8,128)(2,1)} %emb_ref.1, s32[1,512]{1,0:T(1,128)} %bitcast.5, bf16[2,512]{1,0:T(2,128)(2,1)} %place_ref.1, f32[4]{0:T(128)} %scales_ref.1, bf16[512,512]{1,0:T(8,128)(2,1)} %w1_hbm.1, f32[1,512]{1,0:T(1,128)} %bitcast.6, ...), custom_call_target="tpu_custom_call" | custom-call | tf_op jit(solution)/shard_map/pallas_call | solution.py:558
  82.4 1.3 %slice.7 = f32[1,512]{1,0:T(1,128)} slice(f32[40,512]{1,0:T(8,128)} %get-tuple-element.7), slice={[32:33], [0:512]} | slice | bytes 4096 | tf_op jit(solution)/shard_map/slice | solution.py:593
  83.7 1.5 %slice.6 = f32[32,512]{1,0:T(8,128)} slice(f32[40,512]{1,0:T(8,128)} %get-tuple-element.7), slice={[0:32], [0:512]} | slice | bytes 131072 | tf_op jit(solution)/shard_map/slice | solution.py:593
  85.2 0.0 copy-start
  85.2 2.2 %convert_element_type.6 = f32[512,512]{1,0:T(8,128)} convert(bf16[512,512]{1,0:T(8,128)(2,1)} %get-tuple-element.8) | non-fusion elementwise | flops 262144 | bytes 1572864 | tf_op jit(solution)/shard_map/convert_element_type | solution.py:593
  87.4 0.0 copy-done
  87.4 1.1 %convert_element_type.7 = f32[512,512]{1,0:T(8,128)} convert(bf16[512,512]{1,0:T(8,128)(2,1)S(1)} %copy-done) | non-fusion elementwise | flops 262144 | bytes 1572864 | tf_op jit(solution)/shard_map/convert_element_type | solution.py:593
Async XLA Ops:
  85.2 2.2 %copy-start = (bf16[512,512]{1,0:T(8,128)(2,1)S(1)}, bf16[512,512]{1,0:T(8,128)(2,1)}, u32[]{:S(2)}) copy-start(bf16[512,512]{1,0:T(8,128)(2,1)} %get-tuple-element.9) | copy-start | bytes 1572868

commit v6 on v5

--- a/solution.py
+++ b/solution.py
@@ -78,21 +78,21 @@
 
     def band_peer(d, carry):
         pl.semaphore_signal(
-            barrier, inc=1, device_id=(lax.rem(me + d, BANDS), rep), device_id_type=MESH
+            barrier, inc=1, device_id=(((me + d) & (BANDS - 1)), rep), device_id_type=MESH
         )
         return carry
 
-    lax.fori_loop(1, BANDS, band_peer, 0)
+    lax.fori_loop(0, 9, lambda g, c: [band_peer(g * 7 + k, c) for k in range(1, 8)][0], 0)
     for d in range(1, REPS):
         pl.semaphore_signal(
-            barrier, inc=1, device_id=(me, lax.rem(rep + d, REPS)), device_id_type=MESH
+            barrier, inc=1, device_id=(me, ((rep + d) & (REPS - 1))), device_id_type=MESH
         )
     return barrier
 
 
 def send_tiles(me, rep, table, landing, send_sem, recv_sem):
     def send(d, carry):
-        peer = lax.rem(me + d, BANDS)
+        peer = ((me + d) & (BANDS - 1))
         pltpu.make_async_remote_copy(
             src_ref=table.at[pl.ds(pl.multiple_of(peer * TILE, TILE), TILE)],
             dst_ref=landing.at[pl.ds(pl.multiple_of(me * TILE, TILE), TILE)],
@@ -103,7 +103,7 @@
         ).start()
         return carry
 
-    lax.fori_loop(1, BANDS, send, 0)
+    lax.fori_loop(0, 9, lambda g, c: [send(g * 7 + k, c) for k in range(1, 8)][0], 0)
 
 
 def tiles_done(me, rep, table, landing, send_sem, recv_sem):
@@ -112,7 +112,7 @@
         dst_ref=landing.at[pl.ds(0, ROWS - TILE)],
         send_sem=send_sem,
         recv_sem=recv_sem,
-        device_id=(lax.rem(me + 1, BANDS), rep),
+        device_id=(((me + 1) & (BANDS - 1)), rep),
         device_id_type=MESH,
     )
 
@@ -207,21 +207,21 @@
 ):
     me = lax.axis_index("band")
     rep = lax.axis_index("rep")
-    core = lax.rem(me, CORES)
-    z = lax.rem(me // CORES, ZS)
-    y = me // (CORES * ZS)
+    core = ((me) & (CORES - 1))
+    z = (me >> 1) & (ZS - 1)
+    y = me >> 4
 
     def core_peer(d):
         return me + 1 - 2 * core, rep
 
     def y_peer(d):
-        return lax.rem(y + d, YS) * (CORES * ZS) + z * CORES + core, rep
+        return ((y + d) & (YS - 1)) * (CORES * ZS) + z * CORES + core, rep
 
     def z_peer(d):
-        return y * (CORES * ZS) + lax.rem(z + d, ZS) * CORES + core, rep
+        return y * (CORES * ZS) + ((z + d) & (ZS - 1)) * CORES + core, rep
 
     def x_peer(d):
-        return me, lax.rem(rep + d, REPS)
+        return me, ((rep + d) & (REPS - 1))
 
     def start(src, dst, send, recv, device):
         copy = pltpu.make_async_remote_copy(
@@ -280,7 +280,7 @@
 
     def to_group(src, src_at, dst, dst_at, send, recv):
         def one(d, carry):
-            j = lax.rem(group_at + d, ZS * REPS)
+            j = ((group_at + d) & (ZS * REPS - 1))
             pltpu.make_async_remote_copy(
                 src_ref=src.at[pl.ds(pl.multiple_of(src_at(j), TILE), TILE)],
                 dst_ref=dst.at[pl.ds(pl.multiple_of(dst_at, TILE), TILE)],
@@ -288,11 +288,12 @@
             ).start()
             return carry
 
-        lax.fori_loop(1, ZS * REPS, one, 0)
+        for d in range(1, ZS * REPS):
+            one(d, 0)
         rows = pl.ds(0, (ZS * REPS - 1) * TILE)
         return pltpu.make_async_remote_copy(
             src_ref=src.at[rows], dst_ref=dst.at[rows], send_sem=send, recv_sem=recv,
-            device_id=group_peer(lax.rem(group_at + 1, ZS * REPS)), device_id_type=MESH,
+            device_id=group_peer(((group_at + 1) & (ZS * REPS - 1))), device_id_type=MESH,
         )
 
     barrier = greet(me, rep)
@@ -320,7 +321,7 @@
     done = tiles_done(me, rep, table, mine, ssem, rsem)
     done.wait_recv()
     def report_piece(half):
-        return lambda k, h: rr_ref.at[lax.rem(rep + k, REPS), pl.ds(half * 512 + h * 256, 256)]
+        return lambda k, h: rr_ref.at[((rep + k) & (REPS - 1)), pl.ds(half * 512 + h * 256, 256)]
 
     forward_first = ring_gather(report_piece(0), (xs, xr), 0, x_peer)
     ident = eye(128)
@@ -409,7 +410,7 @@
     )
     c_copies = []
     for d in (1, 2, 3, 0):
-        k = lax.rem(y + d, YS)
+        k = ((y + d) & (YS - 1))
         c_copies.append(
             start(g0.at[rows_at((1 - core) * YS + k, 512)], in_c.at[rows_at(k, 512)], gs.at[d], gr.at[d], core_peer(1))
         )
@@ -440,7 +441,7 @@
         lax.fori_loop(0, 4, one_group, 0)
         return [
             start(
-                d_out.at[n, lax.rem(rep + d, REPS)], d_in.at[n, d - 1],
+                d_out.at[n, ((rep + d) & (REPS - 1))], d_in.at[n, d - 1],
                 ds.at[n * 3 + d - 1], dr.at[n * 3 + d - 1], x_peer(d),
             )
             for d in range(1, REPS)
@@ -454,7 +455,7 @@
         table2[n * 256 : (n + 1) * 256, :] = jnp.transpose(total).astype(bf16)
 
         def send(j, carry):
-            peer = n * 16 + lax.rem(j + me, 16)
+            peer = n * 16 + ((j + me) & 15)
 
             @pl.when(peer != me)
             def _():
@@ -469,11 +470,11 @@
 
             return carry
 
-        lax.fori_loop(0, 16, send, 0)
+        lax.fori_loop(0, 4, lambda g, c: [send(g * 4 + k, c) for k in range(4)][0], 0)
 
     y_copies = []
     for d, copy in zip((1, 2, 3, 0), c_copies):
-        k = lax.rem(y + d, YS)
+        k = ((y + d) & (YS - 1))
         copy.wait()
         g1[rows_at(k, 512), :] = (
             g0[rows_at(core * YS + k, 512), :].astype(f32) + in_c[rows_at(k, 512), :].astype(f32)
@@ -516,7 +517,7 @@
         return full_ref.at[rows_at(core * YS + k, 512)]
 
     def to_core(d):
-        k = lax.rem(y + YS - d, YS)
+        k = ((y + YS - d) & (YS - 1))
         return start(block(k), block(k), as_.at[3 + d], ar.at[3 + d], core_peer(1))
 
     blocks = [start(block(y), block(y), as_.at[d - 1], ar.at[d - 1], y_peer(d)) for d in range(1, YS)]
@@ -584,7 +585,7 @@
             dma((7,)), dma((7,)), dma((14,)), dma((14,)), dma((7,)), dma((7,)),
         ],
         compiler_params=pltpu.CompilerParams(
-            collective_id=0, has_side_effects=True, vmem_limit_bytes=60 << 20
+            collective_id=0, has_side_effects=True, vmem_limit_bytes=53 << 20
         ),
     )(
         embeddings, route.reshape(1, REPORTS), place, scales,

time: 88.8 us -> 86.9 us (0.979)
  Pallas kernels: 81.8 us -> 80.4 us
  other arithmetic: 3.3 us -> 2.2 us
    unnamed x2 -> x12, local copies, waits for them, and re-layouts: 0.01 us -> 2.12 us
    pallas_call x1, Pallas kernels: 81.8 us -> 80.4 us  [on_device(): pl.pallas_call(grid_kernel, out_shape=[sds((PART + 8, REPORTS), f32), sds...]
    convert_element_type x1, other arithmetic: 2.2 us -> 1.1 us  [on_device(): first.astype(f32)]
where the time goes in v6:
time: 86.9 us; the launch traced here: 86.7 us
  Pallas kernels  80.4 us (93%)
  local copies, waits for them, and re-layouts  3.33 us (4%)
  other arithmetic  2.2 us (3%)
    pallas_call x1, Pallas kernels, on_device(): pl.pallas_call(grid_kernel, out_shape=[sds((PART + 8, REPORTS), f32), sds...  80.4 us
    unnamed x12, local copies, waits for them, and re-layouts  2.12 us

profile of v6, /device:TPU:1, one launch (start us, length us, event | category | flops | bytes accessed | tf_op | source)
XLA Modules:
  0.0 86.7 jit_solution(16382117132078180253)
XLA Ops:
  0.6 0.0 copy-start.2
  0.6 0.0 copy-start.1
  0.7 0.0 copy-start.4
  0.7 0.7 copy-done.2
  1.3 0.0 copy-done.1
  1.3 0.0 copy-done.4
  1.3 0.0 copy-start
  1.3 0.8 copy-done
  2.1 0.0 copy-start.3
  2.1 0.7 copy-done.3
  2.8 80.4 %shard_map.111 = (f32[40,512]{1,0:T(8,128)S(1)}, bf16[512,512]{1,0:T(8,128)(2,1)S(1)}, bf16[512,512]{1,0:T(8,128)(2,1)}) custom-call(bf16[32,512]{1,0:T(8,128)(2,1)S(1)} %copy-done, s32[1,512]{1,0:T(1,128)S(1)} %bitcast.4, bf16[2,512]{1,0:T(2,128)(2,1)S(1)} %copy-done.2, f32[4]{0:T(128)S(1)} %copy-done.4, bf16[512,512]{1,0:T(8,128)(2,1)} %w1_hbm.1, ...), custom_call_target="tpu_custom_call" | custom-call | tf_op jit(solution)/shard_map/pallas_call | solution.py:559
  83.2 0.6 slice.7
  83.8 0.6 slice.6
  84.4 0.0 copy-start.5
  84.4 1.1 %convert_element_type.6 = f32[512,512]{1,0:T(8,128)} convert(bf16[512,512]{1,0:T(8,128)(2,1)S(1)} %get-tuple-element.8) | non-fusion elementwise | flops 262144 | bytes 1572864 | tf_op jit(solution)/shard_map/convert_element_type | solution.py:594
  85.6 0.0 copy-done.5
  85.6 1.1 %convert_element_type.7 = f32[512,512]{1,0:T(8,128)} convert(bf16[512,512]{1,0:T(8,128)(2,1)S(1)} %copy-done.5) | non-fusion elementwise | flops 262144 | bytes 1572864 | tf_op jit(solution)/shard_map/convert_element_type | solution.py:594
Async XLA Ops:
  0.6 0.7 copy-start.2
  0.6 0.7 copy-start.1
  0.7 0.7 copy-start.4
  1.3 0.8 copy-start
  2.1 0.7 copy-start.3
  84.4 1.1 %copy-start.5 = (bf16[512,512]{1,0:T(8,128)(2,1)S(1)}, bf16[512,512]{1,0:T(8,128)(2,1)}, u32[]{:S(2)}) copy-start(bf16[512,512]{1,0:T(8,128)(2,1)} %get-tuple-element.9) | copy-start | bytes 1572868

commit v7 on v6

--- a/solution.py
+++ b/solution.py
@@ -198,7 +198,7 @@
 
 def grid_kernel(
     emb_ref, route_ref, place_ref, scales_ref, w1_hbm, b1_ref, w2_hbm, cot_hbm,
-    eg_ref, first_ref, second_ref,
+    eg_ref, grads_ref, bout_ref,
     table, rr_ref, pick_ref, w1_ref, w2_ref, cot_ref,
     emb_t, expand, base_ref, east_ref, valid_ref, col_ref, rk_ref, mix_ref, rowf_ref, w_ref, acc_ref,
     feat_ref, w1p_ref, w1t_ref, bcol_ref, hid_ref, pg_ref, sg_ref,
@@ -526,8 +526,8 @@
     landing[own, :] = table2[own, :]
     finish(x_bias)
     bias_total = bias_sum(bx, REPS)
-    bias_row = jnp.concatenate([bias_total[c : c + 1, :] for c in range(4)], axis=1)
-    eg_ref[PART : PART + 8, :] = jnp.broadcast_to(bias_row, (8, HID))
+    for c in range(4):
+        bout_ref[:, c * 128 : (c + 1) * 128] = bias_total[c : c + 1, :]
     for d in (1, 3, 2):
         blocks[d - 1].wait()
         crossing.append(to_core(d))
@@ -537,12 +537,10 @@
     gradient = jnp.zeros((PART, REPORTS), f32)
     for s in range(4):
         gradient = gradient + jnp.where(within == float(s), found[s * PART : (s + 1) * PART, :], 0.0)
-    eg_ref[0:PART, :] = gradient
+    eg_ref[...] = gradient
     finish(crossing)
     for c in range(4):
-        lanes = slice(c * 128, (c + 1) * 128)
-        first_ref[:, lanes] = full_ref[c * 1024 : c * 1024 + 512, :]
-        second_ref[:, lanes] = full_ref[c * 1024 + 512 : (c + 1) * 1024, :]
+        grads_ref[:, c * 128 : (c + 1) * 128] = full_ref[c * 1024 : (c + 1) * 1024, :]
 
 
 def sds(shape, dtype):
@@ -556,9 +554,9 @@
     vm = pltpu.VMEM
     in_vmem = pl.BlockSpec(memory_space=pltpu.VMEM)
     anywhere = pl.BlockSpec(memory_space=pl.ANY)
-    gradient, first, second = pl.pallas_call(
+    gradient, grads, bias = pl.pallas_call(
         grid_kernel,
-        out_shape=[sds((PART + 8, REPORTS), f32), sds((512, 512), bf16), sds((512, 512), bf16)],
+        out_shape=[sds((PART, REPORTS), f32), sds((1024, 512), bf16), sds((1, HID), f32)],
         in_specs=[
             in_vmem, in_vmem, in_vmem, pl.BlockSpec(memory_space=pltpu.SMEM),
             anywhere, in_vmem, anywhere, anywhere,
@@ -585,13 +583,13 @@
             dma((7,)), dma((7,)), dma((14,)), dma((14,)), dma((7,)), dma((7,)),
         ],
         compiler_params=pltpu.CompilerParams(
-            collective_id=0, has_side_effects=True, vmem_limit_bytes=53 << 20
+            collective_id=0, has_side_effects=True, vmem_limit_bytes=60 << 20
         ),
     )(
         embeddings, route.reshape(1, REPORTS), place, scales,
         first_weight, first_bias.reshape(1, HID), second_weight, out_cotangent.transpose(1, 0, 2),
     )
-    return (gradient[0:PART], first.astype(f32), gradient[PART], second.astype(f32))
+    return (gradient, grads[0:512].astype(f32), bias.reshape(HID), grads[512:1024].astype(f32))
 
 
 def solution(mesh):

time: 86.9 us -> 86.4 us (level)
  local copies, waits for them, and re-layouts: 3.33 us -> 1.25 us
  Pallas kernels: 80.4 us -> 81.4 us
    slice x2 -> x0, local copies, waits for them, and re-layouts: 1.21 us -> none  [the longest x1 0.63 us: on_device(): gradient[0:PART]]
    pallas_call x1, Pallas kernels: 80.4 us -> 81.4 us  [on_device(): pl.pallas_call(grid_kernel, out_shape=[sds((PART, REPORTS), f32), sds((10...]
    unnamed x12 -> x6, local copies, waits for them, and re-layouts: 2.12 us -> 1.25 us
    convert_element_type x2 -> x1, other arithmetic: 2.2 us -> 2.84 us  [on_device(): grads[512:1024].astype(f32)]
where the time goes in v7:
time: 86.4 us; the launch traced here: 86.2 us
  Pallas kernels  81.4 us (94%)
  other arithmetic  2.84 us (3%)
  local copies, waits for them, and re-layouts  1.25 us (1%)
    pallas_call x1, Pallas kernels, on_device(): pl.pallas_call(grid_kernel, out_shape=[sds((PART, REPORTS), f32), sds((10...  81.4 us
    convert_element_type x1, other arithmetic, on_device(): grads[512:1024].astype(f32)  2.84 us

profile of v7, /device:TPU:1, one launch (start us, length us, event | category | flops | bytes accessed | tf_op | source)
XLA Modules:
  0.0 86.2 jit_solution(2939623772806417976)
XLA Ops:
  0.6 81.4 %shard_map.111 = (f32[32,512]{1,0:T(8,128)}, bf16[1024,512]{1,0:T(8,128)(2,1)}, f32[1,512]{1,0:T(1,128)}) custom-call(bf16[32,512]{1,0:T(8,128)(2,1)} %emb_ref.1, s32[1,512]{1,0:T(1,128)} %bitcast.5, bf16[2,512]{1,0:T(2,128)(2,1)} %place_ref.1, f32[4]{0:T(128)} %scales_ref.1, bf16[512,512]{1,0:T(8,128)(2,1)} %w1_hbm.1, f32[1,512]{1,0:T(1,128)} %bitcast.6, ...), custom_call_target="tpu_custom_call" | custom-call | tf_op jit(solution)/shard_map/pallas_call | solution.py:557
  82.1 0.0 copy-start
  82.1 2.8 %slice_convert_fusion = (f32[512,512]{1,0:T(8,128)}, f32[512,512]{1,0:T(8,128)}) fusion(bf16[1024,512]{1,0:T(8,128)(2,1)} %get-tuple-element.8), kind=kLoop, calls=%fused_computation | loop fusion | flops 524288 | bytes 3145728 | tf_op jit(solution)/shard_map/convert_element_type | solution.py:592
  84.9 0.0 copy-done
  84.9 0.0 copy-start.1
  84.9 0.6 copy.14
  85.5 0.0 copy-done.1
  85.6 0.6 copy.15
Async XLA Ops:
  82.1 2.9 %copy-start = (f32[32,512]{1,0:T(8,128)S(1)}, f32[32,512]{1,0:T(8,128)}, u32[]{:S(2)}) copy-start(f32[32,512]{1,0:T(8,128)} %get-tuple-element.16) | copy-start | bytes 196612
  84.9 0.7 copy-start.1

commit v8 on v7

--- a/solution.py
+++ b/solution.py
@@ -140,7 +140,7 @@
         east_ref[s] = jnp.broadcast_to(east * float(NLON), (8, ROWS))
 
 
-def build_table(emb_ref, place_ref, owner, rank, pick_ref, table):
+def build_table(emb_ref, place_ref, owner, rank, pick_ref, near_ref, table):
     quad = jnp.floor(rank * 0.25)
     within = rank - 4.0 * quad
     key = owner * 5.0 + quad
@@ -163,8 +163,8 @@
         row_key, place_band = row_keys(part * 128, 128)
         pick = one_where(row_key == key)
         pick_ref[rows, :] = pick
-        near = one_where(jnp.abs(place_band - owner) <= 1.0)
-        table[rows, :] = (dot_nt(pick, emb_b) + dot_nt(near, place_b)).astype(bf16)
+        near_ref[rows, :] = one_where(jnp.abs(place_band - owner) <= 1.0)
+    table[...] = (dot_nt(pick_ref[...], emb_b) + dot_nt(near_ref[...], place_b)).astype(bf16)
     return within
 
 
@@ -199,7 +199,7 @@
 def grid_kernel(
     emb_ref, route_ref, place_ref, scales_ref, w1_hbm, b1_ref, w2_hbm, cot_hbm,
     eg_ref, grads_ref, bout_ref,
-    table, rr_ref, pick_ref, w1_ref, w2_ref, cot_ref,
+    table, rr_ref, pick_ref, near_ref, w1_ref, w2_ref, cot_ref,
     emb_t, expand, base_ref, east_ref, valid_ref, col_ref, rk_ref, mix_ref, rowf_ref, w_ref, acc_ref,
     feat_ref, w1p_ref, w1t_ref, bcol_ref, hid_ref, pg_ref, sg_ref,
     d_out, d_in, table2, landing, g0, g1, g2, in_c, in_y, in_g, full_ref, bc, by, bz, bx,
@@ -304,7 +304,7 @@
         held.append(copy)
 
     owner, rank = report_ranks(route_ref)
-    within = build_table(emb_ref, place_ref, owner, rank, pick_ref, table)
+    within = build_table(emb_ref, place_ref, owner, rank, pick_ref, near_ref, table)
     pl.semaphore_wait(barrier, BANDS - 1 + REPS - 1)
     mine = rr_ref.at[rep]
     send_tiles(me, rep, table, mine, ssem, rsem)
@@ -563,7 +563,7 @@
         ],
         out_specs=[in_vmem] * 3,
         scratch_shapes=[
-            vm((ROWS, 128), bf16), vm((REPS, ROWS, 128), bf16), vm((ROWS, REPORTS), bf16),
+            vm((ROWS, 128), bf16), vm((REPS, ROWS, 128), bf16), vm((ROWS, REPORTS), bf16), vm((ROWS, REPORTS), bf16),
             vm((512, HID), bf16), vm((HID, 512), bf16), vm((SUB, 512, NLON), bf16),
             vm((4, CH, ROWS), bf16), vm((128, ROWS), f32),
             vm((4, 16, ROWS), f32), vm((4, 8, ROWS), f32), vm((4, 16, ROWS), f32),

time: 86.4 us -> 86.5 us (level)
  no operation moved by 1% of the time
where the time goes in v8:
time: 86.5 us; the launch traced here: 86.3 us
  Pallas kernels  81.6 us (94%)
  other arithmetic  2.84 us (3%)
  local copies, waits for them, and re-layouts  1.25 us (1%)
    pallas_call x1, Pallas kernels, on_device(): pl.pallas_call(grid_kernel, out_shape=[sds((PART, REPORTS), f32), sds((10...  81.6 us
    convert_element_type x1, other arithmetic, on_device(): grads[512:1024].astype(f32)  2.84 us

profile of v8, /device:TPU:1, one launch (start us, length us, event | category | flops | bytes accessed | tf_op | source)
XLA Modules:
  0.0 86.3 jit_solution(17782938159940116484)
XLA Ops:
  0.6 81.6 %shard_map.111 = (f32[32,512]{1,0:T(8,128)}, bf16[1024,512]{1,0:T(8,128)(2,1)}, f32[1,512]{1,0:T(1,128)}) custom-call(bf16[32,512]{1,0:T(8,128)(2,1)} %emb_ref.1, s32[1,512]{1,0:T(1,128)} %bitcast.5, bf16[2,512]{1,0:T(2,128)(2,1)} %place_ref.1, f32[4]{0:T(128)} %scales_ref.1, bf16[512,512]{1,0:T(8,128)(2,1)} %w1_hbm.1, f32[1,512]{1,0:T(1,128)} %bitcast.6, ...), custom_call_target="tpu_custom_call" | custom-call | tf_op jit(solution)/shard_map/pallas_call | solution.py:557
  82.2 0.0 copy-start
  82.2 2.8 %slice_convert_fusion = (f32[512,512]{1,0:T(8,128)}, f32[512,512]{1,0:T(8,128)}) fusion(bf16[1024,512]{1,0:T(8,128)(2,1)} %get-tuple-element.8), kind=kLoop, calls=%fused_computation | loop fusion | flops 524288 | bytes 3145728 | tf_op jit(solution)/shard_map/convert_element_type | solution.py:592
  85.0 0.0 copy-done
  85.0 0.0 copy-start.1
  85.0 0.6 copy.14
  85.7 0.0 copy-done.1
  85.7 0.6 copy.15
Async XLA Ops:
  82.2 2.9 %copy-start = (f32[32,512]{1,0:T(8,128)S(1)}, f32[32,512]{1,0:T(8,128)}, u32[]{:S(2)}) copy-start(f32[32,512]{1,0:T(8,128)} %get-tuple-element.16) | copy-start | bytes 196612
  85.0 0.7 copy-start.1

commit v9 on v7

--- a/solution.py
+++ b/solution.py
@@ -31,6 +31,14 @@
 GROWS = 4096
 
 
+def hops(k, n):
+    return min(k % n, n - k % n)
+
+
+BANDS_FAR_FIRST = sorted(range(1, BANDS), key=lambda d: -hops(d >> 4, YS) - hops(d >> 1, ZS))
+GROUP_FAR_FIRST = sorted(range(1, ZS * REPS), key=lambda d: -hops(d >> 2, ZS) - hops(d, REPS))
+
+
 def iota(shape, dim):
     return lax.broadcasted_iota(jnp.int32, shape, dim)
 
@@ -103,7 +111,8 @@
         ).start()
         return carry
 
-    lax.fori_loop(0, 9, lambda g, c: [send(g * 7 + k, c) for k in range(1, 8)][0], 0)
+    for d in BANDS_FAR_FIRST:
+        send(d, 0)
 
 
 def tiles_done(me, rep, table, landing, send_sem, recv_sem):
@@ -288,7 +297,7 @@
             ).start()
             return carry
 
-        for d in range(1, ZS * REPS):
+        for d in GROUP_FAR_FIRST:
             one(d, 0)
         rows = pl.ds(0, (ZS * REPS - 1) * TILE)
         return pltpu.make_async_remote_copy(

time: 86.4 us -> 84 us (0.972)
  Pallas kernels: 81.4 us -> 79 us
    pallas_call x1, Pallas kernels: 81.4 us -> 79 us  [on_device(): pl.pallas_call(grid_kernel, out_shape=[sds((PART, REPORTS), f32), sds((10...]
where the time goes in v9:
time: 84 us; the launch traced here: 83.8 us
  Pallas kernels  79 us (94%)
  other arithmetic  2.84 us (3%)
  local copies, waits for them, and re-layouts  1.25 us (1%)
    pallas_call x1, Pallas kernels, on_device(): pl.pallas_call(grid_kernel, out_shape=[sds((PART, REPORTS), f32), sds((10...  79 us
    convert_element_type x1, other arithmetic, on_device(): grads[512:1024].astype(f32)  2.84 us

profile of v9, /device:TPU:1, one launch (start us, length us, event | category | flops | bytes accessed | tf_op | source)
XLA Modules:
  0.0 83.8 jit_solution(1185173739384436233)
XLA Ops:
  0.6 79.0 %shard_map.111 = (f32[32,512]{1,0:T(8,128)}, bf16[1024,512]{1,0:T(8,128)(2,1)}, f32[1,512]{1,0:T(1,128)}) custom-call(bf16[32,512]{1,0:T(8,128)(2,1)} %emb_ref.1, s32[1,512]{1,0:T(1,128)} %bitcast.5, bf16[2,512]{1,0:T(2,128)(2,1)} %place_ref.1, f32[4]{0:T(128)} %scales_ref.1, bf16[512,512]{1,0:T(8,128)(2,1)} %w1_hbm.1, f32[1,512]{1,0:T(1,128)} %bitcast.6, ...), custom_call_target="tpu_custom_call" | custom-call | tf_op jit(solution)/shard_map/pallas_call | solution.py:566
  79.7 0.0 copy-start
  79.7 2.8 %slice_convert_fusion = (f32[512,512]{1,0:T(8,128)}, f32[512,512]{1,0:T(8,128)}) fusion(bf16[1024,512]{1,0:T(8,128)(2,1)} %get-tuple-element.8), kind=kLoop, calls=%fused_computation | loop fusion | flops 524288 | bytes 3145728 | tf_op jit(solution)/shard_map/convert_element_type | solution.py:601
  82.5 0.0 copy-done
  82.5 0.0 copy-start.1
  82.5 0.6 copy.14
  83.1 0.0 copy-done.1
  83.2 0.6 copy.15
Async XLA Ops:
  79.7 2.9 %copy-start = (f32[32,512]{1,0:T(8,128)S(1)}, f32[32,512]{1,0:T(8,128)}, u32[]{:S(2)}) copy-start(f32[32,512]{1,0:T(8,128)} %get-tuple-element.16) | copy-start | bytes 196612
  82.5 0.7 copy-start.1
